TPU v7x, 32 devices: a whole 2x2x4 slice. The times are simulated.
32 devices in a mesh: rows: 4 (over x, core), chan: 2 (over y), filt: 4 (over z).
Axes of the slice: x: 2, y: 2, z: 4, core: 2. Of those that a mesh axis runs over, the one named last changes fastest.
Arguments:
- images: bfloat16 [16, 2048, 2048], P('rows', 'chan', 'filt'), may hold values from -6 to 6
- first_weight: bfloat16 [2048, 1024], P('chan', 'filt'), may hold values from -0.125 to 0.125
- group_weight: bfloat16 [3, 3, 32, 1024], P(None, None, None, 'filt'), may hold values from -0.375 to 0.375
- third_weight: bfloat16 [1024, 2048], P('chan', 'filt'), may hold values from -0.1875 to 0.1875
- out_grad: bfloat16 [16, 2048, 2048], P('rows', 'chan', 'filt'), may hold values from -6 to 6
Outputs:
- block_out: bfloat16 [16, 2048, 2048], P('rows', 'chan', 'filt')
- images_grad: float32 [16, 2048, 2048], P('rows', 'chan', 'filt')
- first_grad: float32 [2048, 1024], P('chan', 'filt')
- group_grad: float32 [3, 3, 32, 1024], P(None, None, None, 'filt')
- third_grad: float32 [1024, 2048], P('chan', 'filt')
All inputs are finite; a program needn't handle non-finite values.
Results may differ from a plain program's by a relative error of at most 0.006.
Values may be sent and summed in bfloat16 or wider, within the bound.
A program may use at most 192 MiB of HBM per device.

v0:
```python
import jax
import jax.numpy as jnp
from jax import lax
from jax.sharding import PartitionSpec as P


def extended(block, sides, width):
    for axis, dim in sides:
        count = lax.axis_size(axis)
        forward = [(i, i + 1) for i in range(count - 1)]
        backward = [(target, source) for source, target in forward]
        low = lax.ppermute(
            lax.slice_in_dim(block, block.shape[dim] - width, None, axis=dim), axis, forward
        )
        high = lax.ppermute(lax.slice_in_dim(block, 0, width, axis=dim), axis, backward)
        block = jnp.concatenate([low, block, high], axis=dim)
    return block


def silu_slope(values):
    logistic = jax.nn.sigmoid(values)
    return logistic * (1.0 + values * (1.0 - logistic))


def group_conv(padded, kernel, groups_here):
    result = lax.conv_general_dilated(
        padded[None],
        kernel,
        (1, 1),
        "VALID",
        dimension_numbers=("NHWC", "HWIO", "NHWC"),
        feature_group_count=groups_here,
        preferred_element_type=jnp.float32,
    )
    return result[0]


def transposed_kernel(kernel, group_size, groups_here):
    pieces = kernel.reshape(3, 3, group_size, groups_here, group_size)
    swapped = jnp.transpose(pieces, (0, 1, 4, 3, 2)).reshape(
        3, 3, group_size, groups_here * group_size
    )
    return swapped[::-1, ::-1]


def kernel_partial(padded_first, group_delta, group_size, groups_here):
    rows_here = group_delta.shape[0]
    cols_here = group_delta.shape[1]
    pixels = rows_here * cols_here
    delta_groups = group_delta.reshape(pixels, groups_here, group_size)
    kernel_terms = []
    for row_shift in range(3):
        for col_shift in range(3):
            window = padded_first[
                row_shift : row_shift + rows_here, col_shift : col_shift + cols_here
            ]
            window = window.reshape(pixels, groups_here, group_size)
            kernel_terms.append(
                jnp.einsum("pgi,pgo->gio", window, delta_groups, preferred_element_type=jnp.float32)
            )
    kernel_part = jnp.stack(kernel_terms).reshape(3, 3, groups_here, group_size, group_size)
    kernel_part = jnp.transpose(kernel_part, (0, 1, 3, 2, 4))
    return kernel_part.reshape(3, 3, group_size, groups_here * group_size)


def body(images, first_weight, group_weight, third_weight, out_grad):
    rows_here = images.shape[0]
    cols_here = images.shape[1]
    group_size = group_weight.shape[2]
    first_panel, third_panel = (
        lax.all_gather(first_weight, "chan", axis=0, tiled=True),
        lax.all_gather(third_weight, "chan", axis=0, tiled=True),
    )
    pixels = rows_here * cols_here
    groups_here = group_weight.shape[3] // group_size
    gathered = lax.all_gather(images, "filt", axis=2, tiled=True)
    flat_images = gathered.reshape(pixels, gathered.shape[2])
    pre_first = jnp.dot(flat_images, first_panel, preferred_element_type=jnp.float32)
    act_first = (
        jax.nn.silu(pre_first)
        .astype(jnp.bfloat16)
        .reshape(rows_here, cols_here, first_panel.shape[1])
    )
    padded_first = extended(act_first, (("rows", 0), ("chan", 1)), 1)
    pre_group = group_conv(padded_first, group_weight, groups_here)
    act_group = jax.nn.silu(pre_group).astype(jnp.bfloat16)
    mid_whole = lax.all_gather(act_group, "filt", axis=2, tiled=True)
    flat_mid = mid_whole.reshape(pixels, mid_whole.shape[2])
    third_out = jnp.dot(flat_mid, third_panel, preferred_element_type=jnp.float32)
    own_images = images.reshape(pixels, images.shape[2]).astype(jnp.float32)
    block_out = (own_images + third_out).astype(jnp.bfloat16).reshape(images.shape)
    grad_flat = out_grad.reshape(pixels, out_grad.shape[2])
    mid_terms = lax.dot_general(
        grad_flat, third_panel, (((1,), (1,)), ((), ())), preferred_element_type=jnp.float32
    )
    mid_grad = lax.psum_scatter(
        mid_terms.reshape(rows_here, cols_here, mid_terms.shape[1]),
        "filt",
        scatter_dimension=2,
        tiled=True,
    )
    third_part = lax.dot_general(
        flat_mid, grad_flat, (((0,), (0,)), ((), ())), preferred_element_type=jnp.float32
    )
    group_delta = (mid_grad * silu_slope(pre_group)).astype(jnp.bfloat16)
    padded_delta = extended(group_delta, (("rows", 0), ("chan", 1)), 1)
    first_back = group_conv(
        padded_delta, transposed_kernel(group_weight, group_size, groups_here), groups_here
    )
    kernel_part = kernel_partial(padded_first, group_delta, group_size, groups_here)
    first_delta = (first_back.reshape(pixels, first_back.shape[2]) * silu_slope(pre_first)).astype(
        jnp.bfloat16
    )
    first_part = lax.dot_general(
        flat_images, first_delta, (((0,), (0,)), ((), ())), preferred_element_type=jnp.float32
    )
    input_terms = lax.dot_general(
        first_delta, first_panel, (((1,), (1,)), ((), ())), preferred_element_type=jnp.float32
    )
    back_images = lax.psum_scatter(
        input_terms.reshape(rows_here, cols_here, input_terms.shape[1]).astype(jnp.bfloat16),
        "filt",
        scatter_dimension=2,
        tiled=True,
    ).astype(jnp.float32)
    images_grad = out_grad.astype(jnp.float32) + back_images
    group_grad = lax.psum(kernel_part, ("rows", "chan"))
    first_total, third_total = lax.psum((first_part, third_part), "rows")
    first_grad, third_grad = (
        lax.psum_scatter(first_total, "chan", scatter_dimension=0, tiled=True),
        lax.psum_scatter(third_total, "chan", scatter_dimension=0, tiled=True),
    )
    return (block_out, images_grad, first_grad, group_grad, third_grad)


def solution(mesh):
    in_specs = (
        P("rows", "chan", "filt"),
        P("chan", "filt"),
        P(None, None, None, "filt"),
        P("chan", "filt"),
        P("rows", "chan", "filt"),
    )
    out_specs = (
        P("rows", "chan", "filt"),
        P("rows", "chan", "filt"),
        P("chan", "filt"),
        P(None, None, None, "filt"),
        P("chan", "filt"),
    )
    return jax.shard_map(body, mesh=mesh, in_specs=in_specs, out_specs=out_specs, check_vma=False)
```

profile of v0, /device:TPU:0, one launch (start us, length us, event | category | flops | bytes accessed | tf_op | source)
XLA Modules:
  0.0 1346.1 jit_solution(9862081095791899020)
XLA Ops:
  9.4 24.2 %all-gather.11.cloned.1.call-done = bf16[1024,512]{1,0:T(8,128)(2,1)} async-done(((bf16[512,512]{1,0:T(8,128)(2,1)}), bf16[1024,512]{1,0:T(8,128)(2,1)}) %all-gather.11.cloned.1.call-update) | async-done | bytes 1048592 | tf_op jit(solution)/shard_map/all_gather | solution.py:72
  33.6 13.0 fusion.10
  46.7 9.8 all-gather.7.cloned.1.call-done
  56.5 288.4 %all-gather.5.cloned.1.call-done = bf16[4,1024,2048]{2,1,0:T(8,128)(2,1)} async-done(((bf16[4,1024,512]{2,1,0:T(8,128)(2,1)}), bf16[4,1024,2048]{2,1,0:T(8,128)(2,1)}) %all-gather.5.cloned.1.call-update) | async-done | bytes 16777232 | tf_op jit(solution)/shard_map/all_gather | solution.py:76
  344.9 13.1 multiply_convert_fusion.3
  371.2 3.4 collective-permute-start.2
  380.2 4.4 collective-permute-done.3
  384.6 6.6 concatenate.29
  391.2 56.6 %copy.36 = bf16[1,6,1026,8,32]{4,0,3,2,1:T(2,128)(2,1)} copy(bf16[1,6,1026,8,32]{2,4,3,1,0:T(8,128)(2,1)} %bitcast.127) | data formatting | bytes 6303744 | tf_op jit(solution)/shard_map/broadcast_in_dim | solution.py:27
  447.8 69.2 %fusion.13 = f32[1,4,1024,8,32]{4,0,3,2,1:T(1,128)} fusion(bf16[1,6,1026,8,32]{4,0,3,2,1:T(2,128)(2,1)} %copy.36, bf16[3,3,32,8,32]{4,3,2,1,0:T(8,128)(2,1)S(1)} %copy-done.8), kind=kOutput, calls=%fused_computation.40 | convolution fusion | flops 603979776 | bytes 7493632 | tf_op jit(solution)/shard_map/conv_general_dilated | solution.py:26
  517.0 37.5 %copy.38 = f32[1,4,1024,8,32]{2,4,3,1,0:T(8,128)} copy(f32[1,4,1024,8,32]{4,0,3,2,1:T(1,128)} %fusion.13) | data formatting | bytes 8388608 | tf_op jit(solution)/shard_map/conv_general_dilated | solution.py:26
  554.6 5.5 copy.40
  560.1 65.5 %reduce-scatter.5.cloned.1.call-done = f32[4,1024,256]{2,1,0:T(8,128)} async-done(((f32[4,1024,1024]{2,1,0:T(8,128)}), f32[4,1024,256]{2,1,0:T(8,128)}) %reduce-scatter.5.cloned.1.call-update) | async-done | bytes 4194320 | tf_op jit(solution)/shard_map/reduce_scatter | solution.py:96
  625.6 5.3 multiply_convert_fusion.1
  634.1 3.7 collective-permute-done.5
  638.2 3.4 collective-permute-start.6
  647.9 16.7 %concatenate.31 = bf16[6,1026,256]{2,1,0:T(8,128)(2,1)} concatenate(bf16[6,1,256]{2,1,0:T(2,128)(2,1)S(1)} %collective-permute-done.6, bf16[6,1024,256]{2,1,0:T(8,128)(2,1)S(1)} %pad_maximum_fusion.2, bf16[6,1,256]{2,1,0:T(2,128)(2,1)S(1)} %collective-permute-done.7), dimensions={1} | concatenate | bytes 6303744 | tf_op jit(solution)/shard_map/concatenate | solution.py:16
  664.6 4.2 copy.42
  668.8 46.5 %copy.44 = bf16[1,6,1026,8,32]{4,0,3,2,1:T(2,128)(2,1)} copy(bf16[1,6,1026,8,32]{2,4,3,1,0:T(8,128)(2,1)S(1)} %bitcast.128) | data formatting | bytes 6303744 | tf_op jit(solution)/shard_map/broadcast_in_dim | solution.py:27
  715.3 125.4 %convolution_reduce_fusion = f32[4,1024,8,32]{3,2,1,0:T(8,128)} fusion(bf16[1,6,1026,8,32]{4,0,3,2,1:T(2,128)(2,1)} %copy.44, bf16[3,3,32,8,32]{4,3,2,1,0:T(8,128)(2,1)} %rev.6), kind=kOutput, calls=%fused_computation.4 | convolution fusion | flops 603979776 | bytes 7493632 | tf_op jit(solution)/shard_map/conv_general_dilated | solution.py:26
  840.7 12.6 reshape.99
  853.2 4.8 multiply_convert_fusion
  858.1 9.5 convolution_bitcast_fusion
  867.6 10.4 convolution_bitcast_fusion.1
  878.1 28.7 %reduce-scatter.9.cloned.1.call-done = f32[1024,256]{0,1:T(8,128)} async-done(((f32[2048,256]{0,1:T(8,128)}), f32[1024,256]{0,1:T(8,128)}) %reduce-scatter.9.cloned.1.call-update) | async-done | bytes 1048592 | tf_op jit(solution)/shard_map/reduce_scatter | solution.py:130
  906.8 34.7 %reduce-scatter.11.cloned.1.call-done = f32[512,512]{1,0:T(8,128)} async-done(((f32[1024,512]{1,0:T(8,128)}), f32[512,512]{1,0:T(8,128)}) %reduce-scatter.11.cloned.1.call-update) | async-done | bytes 1048592 | tf_op jit(solution)/shard_map/reduce_scatter | solution.py:131
  941.6 8.4 convolution_convert_fusion
  951.7 3.1 copy.53
  957.1 4.6 copy.50
  961.7 4.7 reshape.87
  969.4 4.6 reshape.92
  974.1 3.8 pad_maximum_fusion
  977.8 5.2 fusion.15
  986.1 4.5 reshape.85
  990.6 4.5 copy.51
  995.1 4.5 reshape.88
  999.6 4.5 copy.52
  1004.2 4.8 reshape.89
  1008.9 4.5 copy.54
  1013.5 4.5 reshape.90
  1018.0 4.6 copy.55
  1022.5 4.5 reshape.91
  1030.0 4.6 reshape.93
  1037.7 4.8 reshape.86
  1059.1 10.1 fusion
  1071.8 206.7 %reduce-scatter.7.cloned.1.call-done = bf16[4,1024,512]{2,1,0:T(8,128)(2,1)} async-done(((bf16[4,1024,2048]{2,1,0:T(8,128)(2,1)}), bf16[4,1024,512]{2,1,0:T(8,128)(2,1)}) %reduce-scatter.7.cloned.1.call-update) | async-done | bytes 4194320 | tf_op jit(solution)/shard_map/reduce_scatter | solution.py:120
  1278.5 8.2 convert_add_fusion.1
  1286.7 49.5 %all-reduce.4.cloned.1.call-done = f32[3,3,32,256]{3,2,1,0:T(8,128)} async-done(((f32[3,3,32,256]{3,2,1,0:T(8,128)}), f32[3,3,32,256]{3,2,1,0:T(8,128)}) %all-reduce.4.cloned.1.call-update) | async-done | bytes 294928 | tf_op jit(solution)/shard_map/psum | solution.py:127
  (123 shorter events, 68.9 us)
Async XLA Ops:
  7.2 26.4 %all-gather.11.cloned.1.call-start = ((), (), s32[]{:S(2)}) async-start(), calls=%async_computation.7 | async-start | bytes 1572864 | tf_op jit(solution)/shard_map/all_gather | solution.py:72
  7.9 48.6 %all-gather.7.cloned.1.call-start = ((), (), s32[]{:S(2)}) async-start(), calls=%async_computation.5 | async-start | bytes 1572864 | tf_op jit(solution)/shard_map/all_gather | solution.py:71
  8.6 336.2 %all-gather.5.cloned.1.call-start = ((), (), s32[]{:S(2)}) async-start(), calls=%async_computation.4 | async-start | bytes 20971520 | tf_op jit(solution)/shard_map/all_gather | solution.py:76
  9.4 616.2 %reduce-scatter.5.cloned.1.call-start = ((), (), s32[]{:S(2)}) async-start(), calls=%async_computation.8 | async-start | bytes 20971520 | tf_op jit(solution)/shard_map/reduce_scatter | solution.py:96
  46.6 821.0 %all-gather.9.cloned.1.call-start = ((), (), s32[]{:S(2)}) async-start(), calls=%async_computation.6 | async-start | bytes 10485760 | tf_op jit(solution)/shard_map/all_gather | solution.py:87
  357.9 6.9 copy-start
  359.1 5.8 collective-permute-start
  361.1 5.0 collective-permute-start.1
  364.8 1.3 copy-start.9
  366.1 0.8 copy-start.11
  371.2 9.0 collective-permute-start.2
  374.6 10.0 collective-permute-start.3
  380.2 11.0 copy-start.23
  391.2 56.6 %copy-start.8 = (bf16[3,3,32,8,32]{4,3,2,1,0:T(8,128)(2,1)S(1)}, bf16[3,3,32,8,32]{4,3,2,1,0:T(8,128)(2,1)}, u32[]{:S(2)}) copy-start(bf16[3,3,32,8,32]{4,3,2,1,0:T(8,128)(2,1)} %shard_map.94) | copy-start | bytes 442372
  630.9 7.3 copy-start.2
  631.0 3.1 collective-permute-start.4
  632.6 5.2 collective-permute-start.5
  638.2 9.7 collective-permute-start.6
  641.5 6.3 collective-permute-start.7
  647.8 259.0 %reduce-scatter.9.cloned.1.call-start = ((), (), s32[]{:S(2)}) async-start(), calls=%async_computation.11 | async-start | bytes 3145728 | tf_op jit(solution)/shard_map/reduce_scatter | solution.py:130
  867.6 74.0 %reduce-scatter.11.cloned.1.call-start = ((), (), s32[]{:S(2)}) async-start(), calls=%async_computation.12 | async-start | bytes 3145728 | tf_op jit(solution)/shard_map/reduce_scatter | solution.py:131
  878.1 63.5 %copy-start.26 = (bf16[2048,256]{1,0:T(8,128)(2,1)S(1)}, bf16[2048,256]{1,0:T(8,128)(2,1)}, u32[]{:S(2)}) copy-start(bf16[2048,256]{1,0:T(8,128)(2,1)} %all-gather.7.cloned.1.call-done) | copy-start | bytes 3145732
  878.1 191.1 %all-reduce.6.cloned.1.call-start = ((), (), s32[]{:S(2)}) async-start(), calls=%async_computation.13 | async-start | bytes 4194304 | tf_op jit(solution)/shard_map/psum | solution.py:128
  941.6 336.9 %reduce-scatter.7.cloned.1.call-start = ((), (), s32[]{:S(2)}) async-start(), calls=%async_computation.9 | async-start | bytes 20971520 | tf_op jit(solution)/shard_map/reduce_scatter | solution.py:120
  950.1 1.6 copy-start.1
  950.1 4.7 copy-start.10
  950.1 4.7 copy-start.12
  950.1 386.0 %all-reduce.4.cloned.1.call-start = ((), (), s32[]{:S(2)}) async-start(), calls=%async_computation.10 | async-start | bytes 589824 | tf_op jit(solution)/shard_map/psum | solution.py:127
  961.7 4.7 copy-start.5
  969.4 4.6 copy-start.4
  969.4 4.6 copy-start.6
  969.4 4.6 copy-start.7
  969.4 4.6 copy-start.24
  1030.0 4.6 copy-start.3
  1037.7 4.8 copy-start.20
  1042.5 2.4 copy-start.15
  1042.5 2.9 copy-start.22
  1045.4 1.6 copy-start.18
  1047.0 1.6 copy-start.21
  1048.6 1.6 copy-start.13
  1050.2 1.6 copy-start.16
  1051.8 1.6 copy-start.19
  1053.4 1.6 copy-start.14
  1055.0 1.6 copy-start.17
  1057.3 1.8 copy-start.25
  1071.8 266.1 %copy-start.27 = (f32[512,512]{1,0:T(8,128)S(1)}, f32[512,512]{1,0:T(8,128)}, u32[]{:S(2)}) copy-start(f32[512,512]{1,0:T(8,128)} %get-tuple-element.46) | copy-start | bytes 3145732
Sparse Core Ops, SparseCore 0:
  9.5 23.9 all-gather.10
  35.1 21.2 all-gather.6
  58.0 286.7 all-gather.4
  347.1 278.4 reduce-scatter.4
  647.9 156.4 all-gather.8
  867.7 39.1 reduce-scatter.8
  909.7 31.8 reduce-scatter.10
  944.1 51.5 all-reduce.5
  998.1 280.3 reduce-scatter.6
  1282.3 53.7 all-reduce.3
where the time goes:
time: 1360 us; the launch traced here: 1350 us
  waiting for transfers between devices  720 us (53%)
  local copies, waits for them, and re-layouts  301 us (22%)
  matrix products  267 us (20%)
  other arithmetic  27 us (2%)
  starting transfers between devices  16.1 us (1%)
  between operations  14.9 us (1%)
    all_gather x1, waiting for transfers between devices, body(): gathered = lax.all_gather(images, 'filt', axis=2, tiled=True)  288 us
    reduce_scatter x1, waiting for transfers between devices, body(): lax.psum_scatter(input_terms.reshape(rows_here, cols_here, input_terms.sh...  207 us
    conv_general_dilated x2, matrix products, group_conv(): lax.conv_general_dilated(padded[None], kernel, (1, 1), 'VALID', dimension...  195 us
    broadcast_in_dim x2, local copies, waits for them, and re-layouts, group_conv(): padded[None]  103 us
    reduce_scatter x1, waiting for transfers between devices, body(): lax.psum_scatter(mid_terms.reshape(rows_here, cols_here, mid_terms.shape[...  65.5 us
    psum x1, waiting for transfers between devices, body(): group_grad = lax.psum(kernel_part, ('rows', 'chan'))  49.5 us
    conv_general_dilated x1, local copies, waits for them, and re-layouts, group_conv(): lax.conv_general_dilated(padded[None], kernel, (1, 1), 'VALID', dimension...  37.5 us
    slice x9, local copies, waits for them, and re-layouts, kernel_partial(): padded_first[row_shift:row_shift + rows_here, col_shift:col_shift + cols_...  36.9 us
  transfers between devices with their start and end apart: 18, of which 13 were waited for; matrix products, arithmetic and copies ran while one was open for 43% of the time, Pallas kernels for 0%

commit v1 on v0

v1 whole, which is shorter than its diff:
```python
import jax
import jax.numpy as jnp
from jax import lax
from jax.experimental import pallas as pl
from jax.experimental.pallas import tpu as pltpu
from jax.sharding import PartitionSpec as P

BLOCK = 256
TAPS = [(a, b) for a in range(3) for b in range(3)]


def silu_slope(values):
    logistic = jax.nn.sigmoid(values)
    return logistic * (1.0 + values * (1.0 - logistic))


def to_pixels(block):
    count = lax.axis_size("filt")
    me = lax.axis_index("filt")
    rows, cols, chans = block.shape
    share = cols // count
    out = jnp.zeros((rows, share, chans * count), block.dtype)
    for step in range(count):
        target = lax.rem(me + step, count)
        piece = lax.dynamic_slice(block, (0, target * share, 0), (rows, share, chans))
        if step:
            piece = lax.ppermute(piece, "filt", [(i, (i + step) % count) for i in range(count)])
        source = lax.rem(me + count - step, count)
        out = lax.dynamic_update_slice(out, piece, (0, 0, source * chans))
    return out


def sent_back(block):
    count = lax.axis_size("filt")
    me = lax.axis_index("filt")
    rows, share, whole = block.shape
    chans = whole // count
    pieces = []
    for step in range(count):
        target = lax.rem(me + step, count)
        piece = lax.dynamic_slice(block, (0, 0, target * chans), (rows, share, chans))
        if step:
            piece = lax.ppermute(piece, "filt", [(i, (i + step) % count) for i in range(count)])
        pieces.append(piece)
    return pieces


def hold(pieces, step, *values):
    if step >= len(pieces):
        return values
    pieces[step], *values = lax.optimization_barrier((pieces[step], *values))
    return values


def placed(pieces):
    count = lax.axis_size("filt")
    me = lax.axis_index("filt")
    rows, share, chans = pieces[0].shape
    out = jnp.zeros((rows, share * count, chans), pieces[0].dtype)
    for step, piece in enumerate(pieces):
        source = lax.rem(me + count - step, count)
        out = lax.dynamic_update_slice(out, piece, (0, source * share, 0))
    return out


def whole_weight(shard):
    part = shard.shape[0] // lax.axis_size("rows")
    piece = lax.dynamic_slice_in_dim(shard, lax.axis_index("rows") * part, part, axis=0)
    piece = lax.all_gather(piece, "filt", axis=1, tiled=True)
    return lax.all_gather(piece, ("chan", "rows"), axis=0, tiled=True)


def summed_rows(partial):
    rows, chan = lax.axis_size("rows"), lax.axis_size("chan")
    part = partial.shape[0] // (rows * chan)
    split = partial.astype(jnp.bfloat16).reshape(chan, rows, part, partial.shape[1])
    split = split.swapaxes(0, 1).reshape(partial.shape)
    return lax.psum_scatter(split, "rows", scatter_dimension=0, tiled=True)


def column_windows(block):
    def edges(first, last, axis):
        count = lax.axis_size(axis)
        forward = [(i, i + 1) for i in range(count - 1)]
        backward = [(i + 1, i) for i in range(count - 1)]
        return lax.ppermute(last, axis, forward), lax.ppermute(first, axis, backward)

    low, high = edges(block[:1], block[-1:], "rows")
    tall = jnp.concatenate([low, block, high], axis=0)
    left, right = edges(tall[:, :1], tall[:, -1:], ("chan", "filt"))
    return (
        jnp.concatenate([left, tall[:, :-1]], axis=1),
        tall,
        jnp.concatenate([tall[:, 1:], right], axis=1),
    )


def block_kernels(kernel):
    group_size, mid = kernel.shape[2:]
    count = mid // BLOCK
    pieces = kernel.reshape(9, group_size, count, BLOCK).transpose(2, 0, 1, 3)
    tiled = jnp.tile(pieces, (1, 1, BLOCK // group_size, 1))
    group = jnp.arange(BLOCK) // group_size
    panels = jnp.where(group[:, None] == group[None, :], tiled, jnp.zeros_like(tiled))
    turned = panels.swapaxes(2, 3)
    return panels.reshape(count, 9 * BLOCK, BLOCK), turned.reshape(count, 9 * BLOCK, BLOCK)


def forward_kernel(s0, s1, s2, panel, pre_ref, act_ref):
    shifted = (s0, s1, s2)
    rows, cols = s0.shape[0] - 2, s0.shape[1]
    for i in range(rows):
        wide = jnp.concatenate([shifted[b][i + a] for a, b in TAPS], axis=1)
        pre = jnp.dot(wide, panel[0], preferred_element_type=jnp.float32)
        pre_ref[i * cols : (i + 1) * cols, :] = pre
        act_ref[i * cols : (i + 1) * cols, :] = jax.nn.silu(pre).astype(jnp.bfloat16)


def backward_kernel(group_size, s0, s1, s2, d0, d1, d2, panel, pre_ref, delta_ref, grad_ref):
    shifted, deltas = (s0, s1, s2), (d0, d1, d2)
    rows, cols = s0.shape[0] - 2, s0.shape[1]
    for i in range(rows):
        wide = jnp.concatenate([deltas[2 - b][i + 2 - a] for a, b in TAPS], axis=1)
        back = jnp.dot(wide, panel[0], preferred_element_type=jnp.float32)
        here = slice(i * cols, (i + 1) * cols)
        delta_ref[here, :] = (back * silu_slope(pre_ref[here, :])).astype(jnp.bfloat16)
    own = d1[1 : rows + 1].reshape(rows * cols, BLOCK).T
    out_group = lax.broadcasted_iota(jnp.int32, (BLOCK, BLOCK), 0) // group_size
    in_group = lax.broadcasted_iota(jnp.int32, (BLOCK, BLOCK), 1) // group_size
    same = out_group == in_group
    for tap, (a, b) in enumerate(TAPS):
        window = shifted[b][a : a + rows].reshape(rows * cols, BLOCK)
        full = jnp.dot(own, window, preferred_element_type=jnp.float32)
        full = jnp.where(same, full, 0.0)
        grad_ref[tap] = full.reshape(BLOCK // group_size, group_size, BLOCK).sum(axis=0)


def body(images, first_weight, group_weight, third_weight, out_grad):
    group_size = group_weight.shape[2]
    first_panel = whole_weight(first_weight)
    mid = first_panel.shape[1]
    count = mid // BLOCK
    image_pixels = to_pixels(images)
    rows, share, whole = image_pixels.shape
    pixels = rows * share
    out_grad_later, image_pixels = lax.optimization_barrier((out_grad, image_pixels))
    grad_pixels = to_pixels(out_grad_later)
    third_panel = whole_weight(third_weight)
    kernel = lax.all_gather(group_weight, "filt", axis=3, tiled=True)
    panels, turned = block_kernels(kernel)

    flat_images = image_pixels.reshape(pixels, whole)
    pre_first = jnp.dot(flat_images, first_panel, preferred_element_type=jnp.float32)
    act_first = jax.nn.silu(pre_first).astype(jnp.bfloat16).reshape(rows, share, mid)
    windows = column_windows(act_first)

    window_spec = pl.BlockSpec((rows + 2, share, BLOCK), lambda g: (0, 0, g))
    panel_spec = pl.BlockSpec((1, 9 * BLOCK, BLOCK), lambda g: (g, 0, 0))
    flat_spec = pl.BlockSpec((pixels, BLOCK), lambda g: (0, g))
    params = pltpu.CompilerParams(vmem_limit_bytes=40 * 1024 * 1024)
    pre_group, act_group = pl.pallas_call(
        forward_kernel,
        grid=(count,),
        out_shape=(
            jax.ShapeDtypeStruct((pixels, mid), jnp.float32),
            jax.ShapeDtypeStruct((pixels, mid), jnp.bfloat16),
        ),
        in_specs=[window_spec] * 3 + [panel_spec],
        out_specs=(flat_spec, flat_spec),
        compiler_params=params,
        cost_estimate=pl.CostEstimate(
            flops=18 * pixels * mid * BLOCK, bytes_accessed=40 * pixels * mid, transcendentals=0
        ),
    )(*windows, panels)

    third_out = jnp.dot(act_group, third_panel, preferred_element_type=jnp.float32)
    block_pixels = (flat_images.astype(jnp.float32) + third_out).astype(jnp.bfloat16)
    block_pixels, pre_group = lax.optimization_barrier((block_pixels, pre_group))
    block_pieces = sent_back(block_pixels.reshape(rows, share, whole))
    flat_grad = grad_pixels.reshape(pixels, whole)
    mid_grad = lax.dot_general(
        flat_grad, third_panel, (((1,), (1,)), ((), ())), preferred_element_type=jnp.float32
    )
    group_delta = (mid_grad * silu_slope(pre_group)).astype(jnp.bfloat16)
    (group_delta,) = hold(block_pieces, 1, group_delta)
    delta_windows = column_windows(group_delta.reshape(rows, share, mid))
    third_part = lax.dot_general(
        act_group, flat_grad, (((0,), (0,)), ((), ())), preferred_element_type=jnp.float32
    )
    third_sum = summed_rows(third_part).astype(jnp.float32)
    third_sum = lax.psum_scatter(third_sum, "chan", scatter_dimension=0, tiled=True)
    delta_windows = hold(block_pieces, 2, *delta_windows)

    first_delta, kernel_part = pl.pallas_call(
        lambda *refs: backward_kernel(group_size, *refs),
        grid=(count,),
        out_shape=(
            jax.ShapeDtypeStruct((pixels, mid), jnp.bfloat16),
            jax.ShapeDtypeStruct((9, group_size, mid), jnp.float32),
        ),
        in_specs=[window_spec] * 6 + [panel_spec, flat_spec],
        out_specs=(flat_spec, pl.BlockSpec((9, group_size, BLOCK), lambda g: (0, 0, g))),
        compiler_params=params,
        cost_estimate=pl.CostEstimate(
            flops=36 * pixels * mid * BLOCK, bytes_accessed=60 * pixels * mid, transcendentals=0
        ),
    )(*windows, *delta_windows, turned, pre_first)

    (first_delta,) = hold(block_pieces, 3, first_delta)
    block_out = placed(block_pieces)
    first_part = lax.dot_general(
        flat_images, first_delta, (((0,), (0,)), ((), ())), preferred_element_type=jnp.float32
    )
    back_pixels = lax.dot_general(
        first_delta, first_panel, (((1,), (1,)), ((), ())), preferred_element_type=jnp.float32
    ).astype(jnp.bfloat16)
    back_pieces = sent_back(back_pixels.reshape(rows, share, whole))
    kernel_sum = lax.psum_scatter(kernel_part, "filt", scatter_dimension=2, tiled=True)
    first_sum, third_sum, kernel_sum = hold(
        back_pieces, 1, summed_rows(first_part), third_sum, kernel_sum
    )
    first_sum = first_sum.astype(jnp.float32)
    first_sum = lax.psum_scatter(first_sum, "chan", scatter_dimension=0, tiled=True)
    third_sum = lax.psum_scatter(third_sum, "filt", scatter_dimension=1, tiled=True)
    kernel_sum = lax.psum(kernel_sum, ("rows", "chan"))
    first_sum, third_sum = hold(back_pieces, 2, first_sum, third_sum)
    first_sum = lax.psum_scatter(first_sum, "filt", scatter_dimension=1, tiled=True)
    third_grad = lax.all_gather(third_sum, "rows", axis=0, tiled=True)
    first_sum, kernel_sum = hold(back_pieces, 3, first_sum, kernel_sum)
    first_grad = lax.all_gather(first_sum, "rows", axis=0, tiled=True)
    back_images = placed(back_pieces)
    images_grad = out_grad.astype(jnp.float32) + back_images.astype(jnp.float32)

    own_mid = kernel_sum.shape[2]
    group_grad = kernel_sum.reshape(3, 3, group_size, own_mid // group_size, group_size)
    group_grad = group_grad.transpose(0, 1, 4, 3, 2).reshape(3, 3, group_size, own_mid)
    return (block_out, images_grad, first_grad, group_grad, third_grad)


def solution(mesh):
    in_specs = (
        P("rows", "chan", "filt"),
        P("chan", "filt"),
        P(None, None, None, "filt"),
        P("chan", "filt"),
        P("rows", "chan", "filt"),
    )
    out_specs = (
        P("rows", "chan", "filt"),
        P("rows", "chan", "filt"),
        P("chan", "filt"),
        P(None, None, None, "filt"),
        P("chan", "filt"),
    )
    return jax.shard_map(body, mesh=mesh, in_specs=in_specs, out_specs=out_specs, check_vma=False)
```

time: 1360 us -> 775 us (0.57)
  waiting for transfers between devices: 720 us -> 402 us
  local copies, waits for them, and re-layouts: 301 us -> 71.5 us
  matrix products: 267 us -> 43.8 us
  blocking collectives: 0 us -> 122 us
  starting transfers between devices: 16.1 us -> 58.3 us
  Pallas kernels: 0 us -> 24.2 us
    all_gather x4, waiting for transfers between devices: 322 us -> 13.3 us  [the longest x1 7.81 us: body(): third_grad = lax.all_gather(third_sum, 'rows', axis=0, tiled=True)]
    ppermute x8 -> x20, waiting for transfers between devices: 10.6 us -> 267 us  [the longest x6 195 us: sent_back(): lax.ppermute(piece, 'filt', [(i, (i + step) % count) for i in range(count)])]
    reduce_scatter x4 -> x7, waiting for transfers between devices: 336 us -> 91 us  [the longest x1 34 us: body(): lax.psum_scatter(third_sum, 'chan', scatter_dimension=0, tiled=True)]
    conv_general_dilated x2 -> x0, matrix products: 195 us -> none  [group_conv(): lax.conv_general_dilated(padded[None], kernel, (1, 1), 'VALID', dimension...]
    all_gather x0 -> x3, blocking collectives: none -> 122 us  [the longest x1 86.9 us: body(): kernel = lax.all_gather(group_weight, 'filt', axis=3, tiled=True)]
    broadcast_in_dim x2 -> x1, local copies, waits for them, and re-layouts: 103 us -> 0.18 us  [block_kernels(): jnp.where(group[:, None] == group[None, :], tiled, jnp.zeros_like(tiled))]
    reshape x12 -> x4, local copies, waits for them, and re-layouts: 46.5 us -> 2.83 us  [the longest x1 1.25 us: body(): kernel_sum.reshape(3, 3, group_size, own_mid // group_size, group_size)]
    ppermute x8 -> x20, starting transfers between devices: 15.7 us -> 57.5 us  [the longest x6 27 us: to_pixels(): lax.ppermute(piece, 'filt', [(i, (i + step) % count) for i in range(count)])]
  transfers between devices with their start and end apart: 18 -> 32, of which waited for: 13 -> 17; matrix products, arithmetic and copies ran while one was open for 43% -> 17% of each run, Pallas kernels for 0% -> 3%
where the time goes in v1:
time: 775 us; the launch traced here: 766 us
  waiting for transfers between devices  402 us (52%)
  blocking collectives  122 us (16%)
  local copies, waits for them, and re-layouts  71.5 us (9%)
  starting transfers between devices  58.3 us (8%)
  matrix products  43.8 us (6%)
  other arithmetic  29.2 us (4%)
  Pallas kernels  24.2 us (3%)
  between operations  15.2 us (2%)
    ppermute x6, waiting for transfers between devices, sent_back(): lax.ppermute(piece, 'filt', [(i, (i + step) % count) for i in range(count)])  195 us
    all_gather x1, blocking collectives, body(): kernel = lax.all_gather(group_weight, 'filt', axis=3, tiled=True)  86.9 us
    ppermute x6, waiting for transfers between devices, to_pixels(): lax.ppermute(piece, 'filt', [(i, (i + step) % count) for i in range(count)])  59.8 us
    all_gather x2, blocking collectives, whole_weight(): piece = lax.all_gather(piece, 'filt', axis=1, tiled=True)  35 us
    reduce_scatter x1, waiting for transfers between devices, body(): lax.psum_scatter(third_sum, 'chan', scatter_dimension=0, tiled=True)  34 us
    psum x1, waiting for transfers between devices, body(): kernel_sum = lax.psum(kernel_sum, ('rows', 'chan'))  29.9 us
    reduce_scatter x1, waiting for transfers between devices, body(): lax.psum_scatter(first_sum, 'filt', scatter_dimension=1, tiled=True)  29.6 us
    ppermute x6, starting transfers between devices, to_pixels(): lax.ppermute(piece, 'filt', [(i, (i + step) % count) for i in range(count)])  27 us
  transfers between devices with their start and end apart: 32, of which 17 were waited for; matrix products, arithmetic and copies ran while one was open for 17% of the time, Pallas kernels for 3%

profile of v1, /device:TPU:0, one launch (start us, length us, event | category | flops | bytes accessed | tf_op | source)
XLA Modules:
  0.0 766.2 jit_solution(6901974054359899961)
XLA Ops:
  8.2 18.0 %all_gather.21 = bf16[256,1024]{1,0:T(8,128)(2,1)} all-gather(bf16[256,256]{1,0:T(8,128)(2,1)S(1)} %constant_dynamic-slice_fusion.9), channel_id=1, replica_groups=mesh['rows'=4,'chan'=2,'filt'=4] {'filt'}, dimensions={1}, use_global_device_ids=true | all-gather | bytes 655360 | tf_op jit(solution)/shard_map/all_gather | solution.py:69
  27.2 17.0 %all_gather.24 = bf16[128,2048]{1,0:T(8,128)(2,1)} all-gather(bf16[128,512]{1,0:T(8,128)(2,1)S(1)} %constant_dynamic-slice_fusion.8), channel_id=1, replica_groups=mesh['rows'=4,'chan'=2,'filt'=4] {'filt'}, dimensions={1}, use_global_device_ids=true | all-gather | bytes 655360 | tf_op jit(solution)/shard_map/all_gather | solution.py:69
  50.0 2.5 collective-permute-start.1
  53.0 24.1 %collective-permute-done = bf16[4,256,512]{2,1,0:T(8,128)(2,1)} collective-permute-done((bf16[4,256,512]{2,1,0:T(8,128)(2,1)S(1)}, bf16[4,256,512]{2,1,0:T(8,128)(2,1)}, u32[]{:S(2)}, u32[]{:S(2)}) %collective-permute-start) | collective-permute-done | bytes 1048608 | tf_op jit(solution)/shard_map/ppermute | solution.py:27
  79.4 35.7 %collective-permute-done.1 = bf16[4,256,512]{2,1,0:T(8,128)(2,1)} collective-permute-done((bf16[4,256,512]{2,1,0:T(8,128)(2,1)S(1)}, bf16[4,256,512]{2,1,0:T(8,128)(2,1)}, u32[]{:S(2)}, u32[]{:S(2)}) %collective-permute-start.1) | collective-permute-done | bytes 1048608 | tf_op jit(solution)/shard_map/ppermute | solution.py:27
  117.5 2.4 constant_dynamic-update-slice_fusion.9
  124.2 20.6 %collective-permute-start.8 = (bf16[4,256,512]{2,1,0:T(8,128)(2,1)}, bf16[4,256,512]{2,1,0:T(8,128)(2,1)}, u32[]{:S(2)}, u32[]{:S(2)}) collective-permute-start(bf16[4,256,512]{2,1,0:T(8,128)(2,1)} %get-tuple-element.67), channel_id=1, source_target_pairs={{0,1},{1,2},{2,3},{3,0},{4,5},{5,6},{6,7},{7,4},{8,9},{9,10},{10,1... | collective-permute-start | bytes 3145736 | tf_op jit(solution)/shard_map/ppermute | solution.py:27
  144.7 2.5 collective-permute-start.9
  147.3 10.4 %multiply_convert_fusion.1 = (bf16[1024,1024]{1,0:T(8,128)(2,1)S(1)}, f32[1024,1024]{1,0:T(8,128)}) fusion(bf16[1024,2048]{1,0:T(8,128)(2,1)} %bitcast.62, bf16[2048,1024]{1,0:T(8,128)(2,1)} %all-gather.5.cloned.1.call-done), kind=kOutput, calls=%fused_computation.5 | convolution fusion | flops 4300210176 | bytes 14680064 | tf_op jit(solution)/shard_map/dot_general | solution.py:153
  162.1 86.9 %all_gather.23 = bf16[3,3,32,1024]{3,2,1,0:T(8,128)(2,1)S(1)} all-gather(bf16[3,3,32,256]{3,2,1,0:T(8,128)(2,1)S(1)} %copy-done.28), channel_id=1, replica_groups=mesh['rows'=4,'chan'=2,'filt'=4] {'filt'}, dimensions={3}, use_global_device_ids=true | all-gather | bytes 737280 | tf_op jit(solution)/shard_map/all_gather | solution.py:149
  249.8 2.9 bitcast_select_fusion.1.panel
  257.3 2.4 pad_maximum_fusion.s1.refs_1_
  262.6 4.7 collective-permute-start.5
  269.7 9.8 %shard_map.92 = (f32[1024,1024]{1,0:T(8,128)}, bf16[1024,1024]{1,0:T(8,128)(2,1)S(1)}) custom-call(bf16[6,256,1024]{2,1,0:T(8,128)(2,1)S(1)} %pad_maximum_fusion.1.s0.refs_0_, bf16[6,256,1024]{2,1,0:T(8,128)(2,1)S(1)} %pad_maximum_fusion.s1.refs_1_, bf16[6,256,1024]{2,1,0:T(8,128)(2,1)S(1)} %pad_maximum_fusion.2.s2.refs_2_, ...), custom_call_target="tpu_custom_call" | custom-call | flops 4831838208 | bytes 41943040 | tf_op jit(solution)/shard_map/pallas_call | solution.py:161
  280.9 4.8 convolution_convert_fusion
  285.7 2.5 copy.19
  288.3 8.6 %add_convert_fusion = bf16[1024,2048]{1,0:T(8,128)(2,1)S(1)} fusion(bf16[1024,2048]{1,0:T(8,128)(2,1)} %bitcast.63, bf16[1024,1024]{1,0:T(8,128)(2,1)} %copy-done.7, bf16[1024,2048]{1,0:T(8,128)(2,1)} %all-gather.7.cloned.1.call-done), kind=kOutput, calls=%fused_computation.1 | convolution fusion | flops 4301258752 | bytes 14680064 | tf_op jit(solution)/shard_map/dot_general | solution.py:176
  296.9 2.7 broadcast.79.clone
  304.9 5.7 multiply_convert_fusion
  310.6 14.0 %collective-permute-done.7 = bf16[4,256,512]{2,1,0:T(8,128)(2,1)S(1)} collective-permute-done((bf16[4,256,512]{2,1,0:T(8,128)(2,1)S(1)}, bf16[4,256,512]{2,1,0:T(8,128)(2,1)S(1)}, u32[]{:S(2)}, u32[]{:S(2)}) %collective-permute-start.7) | collective-permute-done | bytes 1048608 | tf_op jit(solution)/shard_map/ppermute | solution.py:43
  329.3 2.5 bitcast_select_fusion
  331.8 6.7 copy.17
  343.7 4.6 collective-permute-start.14
  350.5 10.9 %collective-permute-done.14 = bf16[6,1,1024]{2,1,0:T(2,128)(2,1)S(1)} collective-permute-done((bf16[6,1,1024]{2,1,0:T(2,128)(2,1)S(1)}, bf16[6,1,1024]{2,1,0:T(2,128)(2,1)S(1)}, u32[]{:S(2)}, u32[]{:S(2)}) %collective-permute-start.14) | collective-permute-done | bytes 12320 | tf_op jit(solution)/shard_map/ppermute | solution.py:86
  361.4 2.7 pad_maximum_fusion.4.refs_3_
  364.2 23.2 %collective-permute-done.11 = bf16[4,256,512]{2,1,0:T(8,128)(2,1)S(1)} collective-permute-done((bf16[4,256,512]{2,1,0:T(8,128)(2,1)}, bf16[4,256,512]{2,1,0:T(8,128)(2,1)S(1)}, u32[]{:S(2)}, u32[]{:S(2)}) %collective-permute-start.11) | collective-permute-done | bytes 1048608 | tf_op jit(solution)/shard_map/ppermute | solution.py:43
  387.4 14.3 %shard_map.93 = (bf16[1024,1024]{1,0:T(8,128)(2,1)S(1)}, f32[9,32,1024]{2,1,0:T(8,128)S(1)}) custom-call(bf16[6,256,1024]{2,1,0:T(8,128)(2,1)S(1)} %copy-done.5, bf16[6,256,1024]{2,1,0:T(8,128)(2,1)S(1)} %pad_maximum_fusion.s1.refs_1_, bf16[6,256,1024]{2,1,0:T(8,128)(2,1)S(1)} %copy-done.3, bf16[6,256,1024]{2,1,0:T(8,128)(2,1)} %pad_maximum_fusion.4.refs_3_, ...), custom_call_target="tpu_custom_call" | custom-call | flops 9663676416 | bytes 62914560 | tf_op jit(solution)/shard_map/pallas_call | solution.py:194
  406.0 48.4 %collective-permute-done.16 = bf16[4,256,512]{2,1,0:T(8,128)(2,1)S(1)} collective-permute-done((bf16[4,256,512]{2,1,0:T(8,128)(2,1)}, bf16[4,256,512]{2,1,0:T(8,128)(2,1)S(1)}, u32[]{:S(2)}, u32[]{:S(2)}) %collective-permute-start.16) | collective-permute-done | bytes 1048608 | tf_op jit(solution)/shard_map/ppermute | solution.py:43
  454.4 7.5 convolution_convert_fusion.1
  461.9 2.5 copy.18
  464.4 2.9 convert_element_type.41
  467.7 7.0 convolution_convert_fusion.2
  474.6 2.4 broadcast.79
  480.2 24.6 %collective-permute-done.17 = bf16[4,256,512]{2,1,0:T(8,128)(2,1)} collective-permute-done((bf16[4,256,512]{2,1,0:T(8,128)(2,1)S(1)}, bf16[4,256,512]{2,1,0:T(8,128)(2,1)}, u32[]{:S(2)}, u32[]{:S(2)}) %collective-permute-start.17) | collective-permute-done | bytes 1048608 | tf_op jit(solution)/shard_map/ppermute | solution.py:43
  504.8 6.7 reduce-scatter.8.cloned.1.call-done
  511.5 34.0 %reduce-scatter.12.cloned.1.call-done = f32[128,2048]{1,0:T(8,128)} async-done(((f32[256,2048]{1,0:T(8,128)}), f32[128,2048]{1,0:T(8,128)}) %reduce-scatter.12.cloned.1.call-update) | async-done | bytes 1048592 | tf_op jit(solution)/shard_map/reduce_scatter | solution.py:191
  545.6 2.8 convert_element_type.42
  548.4 2.5 collective-permute-start.18
  551.0 62.7 %collective-permute-done.18 = bf16[4,256,512]{2,1,0:T(8,128)(2,1)} collective-permute-done((bf16[4,256,512]{2,1,0:T(8,128)(2,1)S(1)}, bf16[4,256,512]{2,1,0:T(8,128)(2,1)}, u32[]{:S(2)}, u32[]{:S(2)}) %collective-permute-start.18) | collective-permute-done | bytes 1048608 | tf_op jit(solution)/shard_map/ppermute | solution.py:43
  613.7 20.7 %reduce-scatter.16.cloned.1.call-done = f32[256,1024]{1,0:T(8,128)} async-done(((f32[512,1024]{1,0:T(8,128)}), f32[256,1024]{1,0:T(8,128)}) %reduce-scatter.16.cloned.1.call-update) | async-done | bytes 1048592 | tf_op jit(solution)/shard_map/reduce_scatter | solution.py:223
  635.2 3.4 collective-permute-start.19
  638.6 22.4 %collective-permute-done.19 = bf16[4,256,512]{2,1,0:T(8,128)(2,1)S(1)} collective-permute-done((bf16[4,256,512]{2,1,0:T(8,128)(2,1)S(1)}, bf16[4,256,512]{2,1,0:T(8,128)(2,1)S(1)}, u32[]{:S(2)}, u32[]{:S(2)}) %collective-permute-start.19) | collective-permute-done | bytes 1048608 | tf_op jit(solution)/shard_map/ppermute | solution.py:43
  661.0 29.9 %all-reduce.2.cloned.1.call-done = f32[9,32,256]{2,1,0:T(8,128)} async-done(((f32[9,32,256]{2,1,0:T(8,128)}), f32[9,32,256]{2,1,0:T(8,128)}) %all-reduce.2.cloned.1.call-update) | async-done | bytes 294928 | tf_op jit(solution)/shard_map/psum | solution.py:225
  690.9 29.6 %reduce-scatter.20.cloned.1.call-done = f32[256,256]{1,0:T(8,128)} async-done(((f32[256,1024]{1,0:T(8,128)}), f32[256,256]{1,0:T(8,128)}) %reduce-scatter.20.cloned.1.call-update) | async-done | bytes 262160 | tf_op jit(solution)/shard_map/reduce_scatter | solution.py:227
  729.7 7.8 %all-gather.11.cloned.1.call-done = f32[512,512]{1,0:T(8,128)} async-done(((f32[128,512]{1,0:T(8,128)}), f32[512,512]{1,0:T(8,128)}) %all-gather.11.cloned.1.call-update) | async-done | bytes 1048592 | tf_op jit(solution)/shard_map/all_gather | solution.py:228
  740.3 2.9 constant_dynamic-update-slice_fusion.1
  743.2 7.0 convert_add_fusion
  750.2 5.4 all-gather.9.cloned.1.call-done
  (152 shorter events, 74.7 us)
Async XLA Ops:
  7.2 140.1 %all-gather.5.cloned.1.call-start = ((), (), s32[]{:S(2)}) async-start(), calls=%async_computation.7 | async-start | bytes 4718592 | tf_op jit(solution)/shard_map/all_gather | solution.py:70
  26.2 262.1 %all-gather.7.cloned.1.call-start = ((), (), s32[]{:S(2)}) async-start(), calls=%async_computation.8 | async-start | bytes 4718592 | tf_op jit(solution)/shard_map/all_gather | solution.py:70
  44.3 420.1 %reduce-scatter.10.cloned.1.call-start = ((), (), s32[]{:S(2)}) async-start(), calls=%async_computation.10 | async-start | bytes 5242880 | tf_op jit(solution)/shard_map/reduce_scatter | solution.py:78
  49.1 28.1 %collective-permute-start = (bf16[4,256,512]{2,1,0:T(8,128)(2,1)S(1)}, bf16[4,256,512]{2,1,0:T(8,128)(2,1)}, u32[]{:S(2)}, u32[]{:S(2)}) collective-permute-start(bf16[4,256,512]{2,1,0:T(8,128)(2,1)S(1)} %get-tuple-element.70), channel_id=1, source_target_pairs={{0,1},{1,2},{2,3},{3,0},{4,5},{5,6},{6,7},{7,4},{8,9},{9,10},{10,1... | collective-permute-start | bytes 3145736 | tf_op jit(solution)/shard_map/ppermute | solution.py:27
  50.0 65.2 %collective-permute-start.1 = (bf16[4,256,512]{2,1,0:T(8,128)(2,1)S(1)}, bf16[4,256,512]{2,1,0:T(8,128)(2,1)}, u32[]{:S(2)}, u32[]{:S(2)}) collective-permute-start(bf16[4,256,512]{2,1,0:T(8,128)(2,1)S(1)} %get-tuple-element.72), channel_id=1, source_target_pairs={{0,2},{1,3},{2,0},{3,1},{4,6},{5,7},{6,4},{7,5},{8,10},{9,11},{10,... | collective-permute-start | bytes 3145736 | tf_op jit(solution)/shard_map/ppermute | solution.py:27
  52.5 65.0 %collective-permute-start.2 = (bf16[4,256,512]{2,1,0:T(8,128)(2,1)S(1)}, bf16[4,256,512]{2,1,0:T(8,128)(2,1)}, u32[]{:S(2)}, u32[]{:S(2)}) collective-permute-start(bf16[4,256,512]{2,1,0:T(8,128)(2,1)S(1)} %get-tuple-element.69), channel_id=1, source_target_pairs={{0,3},{1,0},{2,1},{3,2},{4,7},{5,4},{6,5},{7,6},{8,11},{9,8},{10,9... | collective-permute-start | bytes 3145736 | tf_op jit(solution)/shard_map/ppermute | solution.py:27
  79.4 40.9 %copy-start.11 = (bf16[4,1024,512]{2,1,0:T(8,128)(2,1)S(1)}, bf16[4,1024,512]{2,1,0:T(8,128)(2,1)}, u32[]{:S(2)}) copy-start(bf16[4,1024,512]{2,1,0:T(8,128)(2,1)} %param.9) | copy-start | bytes 12582916
  124.2 128.6 %collective-permute-start.8 = (bf16[4,256,512]{2,1,0:T(8,128)(2,1)}, bf16[4,256,512]{2,1,0:T(8,128)(2,1)}, u32[]{:S(2)}, u32[]{:S(2)}) collective-permute-start(bf16[4,256,512]{2,1,0:T(8,128)(2,1)} %get-tuple-element.67), channel_id=1, source_target_pairs={{0,1},{1,2},{2,3},{3,0},{4,5},{5,6},{6,7},{7,4},{8,9},{9,10},{10,1... | collective-permute-start | bytes 3145736 | tf_op jit(solution)/shard_map/ppermute | solution.py:27
  144.7 109.7 %collective-permute-start.9 = (bf16[4,256,512]{2,1,0:T(8,128)(2,1)}, bf16[4,256,512]{2,1,0:T(8,128)(2,1)}, u32[]{:S(2)}, u32[]{:S(2)}) collective-permute-start(bf16[4,256,512]{2,1,0:T(8,128)(2,1)} %get-tuple-element.66), channel_id=1, source_target_pairs={{0,2},{1,3},{2,0},{3,1},{4,6},{5,7},{6,4},{7,5},{8,10},{9,11},{10,... | collective-permute-start | bytes 3145736 | tf_op jit(solution)/shard_map/ppermute | solution.py:27
  147.3 108.6 %collective-permute-start.10 = (bf16[4,256,512]{2,1,0:T(8,128)(2,1)}, bf16[4,256,512]{2,1,0:T(8,128)(2,1)}, u32[]{:S(2)}, u32[]{:S(2)}) collective-permute-start(bf16[4,256,512]{2,1,0:T(8,128)(2,1)} %get-tuple-element.65), channel_id=1, source_target_pairs={{0,3},{1,0},{2,1},{3,2},{4,7},{5,4},{6,5},{7,6},{8,11},{9,8},{10,9... | collective-permute-start | bytes 3145736 | tf_op jit(solution)/shard_map/ppermute | solution.py:27
  147.3 14.9 %copy-start.28 = (bf16[3,3,32,256]{3,2,1,0:T(8,128)(2,1)S(1)}, bf16[3,3,32,256]{3,2,1,0:T(8,128)(2,1)}, u32[]{:S(2)}) copy-start(bf16[3,3,32,256]{3,2,1,0:T(8,128)(2,1)} %param.7) | copy-start | bytes 442372
  157.6 95.1 %copy-start.15 = (bf16[1024,1024]{1,0:T(8,128)(2,1)}, bf16[1024,1024]{1,0:T(8,128)(2,1)S(1)}, u32[]{:S(2)}) copy-start(bf16[1024,1024]{1,0:T(8,128)(2,1)S(1)} %get-tuple-element.85) | copy-start | bytes 6291460
  158.7 98.6 %collective-permute-start.3 = (bf16[1,256,1024]{2,1,0:T(8,128)(2,1)}, bf16[1,256,1024]{2,1,0:T(8,128)(2,1)}, u32[]{:S(2)}, u32[]{:S(2)}) collective-permute-start(bf16[1,256,1024]{2,1,0:T(8,128)(2,1)} %get-tuple-element.83), channel_id=1, source_target_pairs={{0,8},{8,16},{16,24},{1,9},{9,17},{17,25},{2,10},{10,18},{18,26},{... | collective-permute-start | bytes 1572872 | tf_op jit(solution)/shard_map/ppermute | solution.py:86
  160.8 96.5 %collective-permute-start.4 = (bf16[1,256,1024]{2,1,0:T(8,128)(2,1)}, bf16[1,256,1024]{2,1,0:T(8,128)(2,1)}, u32[]{:S(2)}, u32[]{:S(2)}) collective-permute-start(bf16[1,256,1024]{2,1,0:T(8,128)(2,1)} %get-tuple-element.84), channel_id=1, source_target_pairs={{8,0},{16,8},{24,16},{9,1},{17,9},{25,17},{10,2},{18,10},{26,18},{... | collective-permute-start | bytes 1572872 | tf_op jit(solution)/shard_map/ppermute | solution.py:86
  257.3 22.3 %copy-start.21 = (bf16[4,256,2048]{2,1,0:T(8,128)(2,1)}, bf16[4,256,2048]{2,1,0:T(8,128)(2,1)S(1)}, u32[]{:S(2)}) copy-start(bf16[4,256,2048]{2,1,0:T(8,128)(2,1)S(1)} %constant_dynamic-update-slice_fusion.5) | copy-start | bytes 12582916
  259.8 7.5 collective-permute-start.6
  262.6 6.1 collective-permute-start.5
  267.7 11.8 %copy-start.2 = (bf16[6,256,1024]{2,1,0:T(8,128)(2,1)}, bf16[6,256,1024]{2,1,0:T(8,128)(2,1)S(1)}, u32[]{:S(2)}) copy-start(bf16[6,256,1024]{2,1,0:T(8,128)(2,1)S(1)} %pad_maximum_fusion.2.s2.refs_2_) | copy-start | bytes 9437188
  269.7 9.8 %copy-start.4 = (bf16[6,256,1024]{2,1,0:T(8,128)(2,1)}, bf16[6,256,1024]{2,1,0:T(8,128)(2,1)S(1)}, u32[]{:S(2)}) copy-start(bf16[6,256,1024]{2,1,0:T(8,128)(2,1)S(1)} %pad_maximum_fusion.1.s0.refs_0_) | copy-start | bytes 9437188
  288.2 216.6 %reduce-scatter.14.cloned.1.call-start = ((), (), s32[]{:S(2)}) async-start(), calls=%async_computation.12 | async-start | bytes 1474560 | tf_op jit(solution)/shard_map/reduce_scatter | solution.py:218
  296.9 7.1 copy-start.30
  301.7 27.5 %copy-start.14 = (bf16[9,32,4,256]{3,1,0,2:T(8,128)(2,1)S(1)}, bf16[9,32,4,256]{3,1,0,2:T(8,128)(2,1)}, u32[]{:S(2)}) copy-start(bf16[9,32,4,256]{3,1,0,2:T(8,128)(2,1)} %copy-done.13) | copy-start | bytes 1769476
  301.8 22.8 %collective-permute-start.7 = (bf16[4,256,512]{2,1,0:T(8,128)(2,1)S(1)}, bf16[4,256,512]{2,1,0:T(8,128)(2,1)S(1)}, u32[]{:S(2)}, u32[]{:S(2)}) collective-permute-start(bf16[4,256,512]{2,1,0:T(8,128)(2,1)S(1)} %get-tuple-element.63), channel_id=1, source_target_pairs={{0,1},{1,2},{2,3},{3,0},{4,5},{5,6},{6,7},{7,4},{8,9},{9,10},{10,1... | collective-permute-start | bytes 3145736 | tf_op jit(solution)/shard_map/ppermute | solution.py:43
  310.6 21.2 %copy-start.17 = (bf16[1024,1024]{1,0:T(8,128)(2,1)}, bf16[1024,1024]{1,0:T(8,128)(2,1)S(1)}, u32[]{:S(2)}) copy-start(bf16[1024,1024]{1,0:T(8,128)(2,1)S(1)} %multiply_convert_fusion) | copy-start | bytes 6291460
  324.6 7.2 copy-start.25
  325.7 13.0 %collective-permute-start.12 = (bf16[1,256,1024]{2,1,0:T(8,128)(2,1)}, bf16[1,256,1024]{2,1,0:T(8,128)(2,1)}, u32[]{:S(2)}, u32[]{:S(2)}) collective-permute-start(bf16[1,256,1024]{2,1,0:T(8,128)(2,1)} %get-tuple-element.81), channel_id=1, source_target_pairs={{0,8},{8,16},{16,24},{1,9},{9,17},{17,25},{2,10},{10,18},{18,26},{... | collective-permute-start | bytes 1572872 | tf_op jit(solution)/shard_map/ppermute | solution.py:86
  327.8 10.9 %collective-permute-start.13 = (bf16[1,256,1024]{2,1,0:T(8,128)(2,1)}, bf16[1,256,1024]{2,1,0:T(8,128)(2,1)}, u32[]{:S(2)}, u32[]{:S(2)}) collective-permute-start(bf16[1,256,1024]{2,1,0:T(8,128)(2,1)} %get-tuple-element.82), channel_id=1, source_target_pairs={{8,0},{16,8},{24,16},{9,1},{17,9},{25,17},{10,2},{18,10},{26,18},{... | collective-permute-start | bytes 1572872 | tf_op jit(solution)/shard_map/ppermute | solution.py:86
  338.5 48.9 %collective-permute-start.11 = (bf16[4,256,512]{2,1,0:T(8,128)(2,1)}, bf16[4,256,512]{2,1,0:T(8,128)(2,1)S(1)}, u32[]{:S(2)}, u32[]{:S(2)}) collective-permute-start(bf16[4,256,512]{2,1,0:T(8,128)(2,1)} %get-tuple-element.62), channel_id=1, source_target_pairs={{0,2},{1,3},{2,0},{3,1},{4,6},{5,7},{6,4},{7,5},{8,10},{9,11},{10,... | collective-permute-start | bytes 3145736 | tf_op jit(solution)/shard_map/ppermute | solution.py:43
  341.0 7.4 collective-permute-start.15
  343.7 17.7 %collective-permute-start.14 = (bf16[6,1,1024]{2,1,0:T(2,128)(2,1)S(1)}, bf16[6,1,1024]{2,1,0:T(2,128)(2,1)S(1)}, u32[]{:S(2)}, u32[]{:S(2)}) collective-permute-start(bf16[6,1,1024]{2,1,0:T(2,128)(2,1)S(1)} %get-tuple-element.76), channel_id=1, source_target_pairs={{0,1},{1,2},{2,3},{3,4},{4,5},{5,6},{6,7},{8,9},{9,10},{10,11},{11... | collective-permute-start | bytes 36872 | tf_op jit(solution)/shard_map/ppermute | solution.py:86
  350.5 36.9 %copy-start.3 = (bf16[6,256,1024]{2,1,0:T(8,128)(2,1)S(1)}, bf16[6,256,1024]{2,1,0:T(8,128)(2,1)}, u32[]{:S(2)}) copy-start(bf16[6,256,1024]{2,1,0:T(8,128)(2,1)} %copy-done.2) | copy-start | bytes 9437188
  350.5 36.9 %copy-start.5 = (bf16[6,256,1024]{2,1,0:T(8,128)(2,1)S(1)}, bf16[6,256,1024]{2,1,0:T(8,128)(2,1)}, u32[]{:S(2)}) copy-start(bf16[6,256,1024]{2,1,0:T(8,128)(2,1)} %copy-done.4) | copy-start | bytes 9437188
  387.4 14.3 %copy-start.26 = (bf16[4,256,512]{2,1,0:T(8,128)(2,1)}, bf16[4,256,512]{2,1,0:T(8,128)(2,1)S(1)}, u32[]{:S(2)}) copy-start(bf16[4,256,512]{2,1,0:T(8,128)(2,1)S(1)} %collective-permute-done.11) | copy-start | bytes 3145732
  404.1 107.4 %reduce-scatter.8.cloned.1.call-start = ((), (), s32[]{:S(2)}) async-start(), calls=%async_computation.9 | async-start | bytes 5242880 | tf_op jit(solution)/shard_map/reduce_scatter | solution.py:78
  404.2 50.2 %collective-permute-start.16 = (bf16[4,256,512]{2,1,0:T(8,128)(2,1)}, bf16[4,256,512]{2,1,0:T(8,128)(2,1)S(1)}, u32[]{:S(2)}, u32[]{:S(2)}) collective-permute-start(bf16[4,256,512]{2,1,0:T(8,128)(2,1)} %get-tuple-element.61), channel_id=1, source_target_pairs={{0,3},{1,0},{2,1},{3,2},{4,7},{5,4},{6,5},{7,6},{8,11},{9,8},{10,9... | collective-permute-start | bytes 3145736 | tf_op jit(solution)/shard_map/ppermute | solution.py:43
  464.3 81.2 %reduce-scatter.12.cloned.1.call-start = ((), (), s32[]{:S(2)}) async-start(), calls=%async_computation.11 | async-start | bytes 3145728 | tf_op jit(solution)/shard_map/reduce_scatter | solution.py:191
  467.3 146.4 %reduce-scatter.18.cloned.1.call-start = ((), (), s32[]{:S(2)}) async-start(), calls=%async_computation.14 | async-start | bytes 1310720 | tf_op jit(solution)/shard_map/reduce_scatter | solution.py:224
  478.5 26.3 %collective-permute-start.17 = (bf16[4,256,512]{2,1,0:T(8,128)(2,1)S(1)}, bf16[4,256,512]{2,1,0:T(8,128)(2,1)}, u32[]{:S(2)}, u32[]{:S(2)}) collective-permute-start(bf16[4,256,512]{2,1,0:T(8,128)(2,1)S(1)} %get-tuple-element.59), channel_id=1, source_target_pairs={{0,1},{1,2},{2,3},{3,0},{4,5},{5,6},{6,7},{7,4},{8,9},{9,10},{10,1... | collective-permute-start | bytes 3145736 | tf_op jit(solution)/shard_map/ppermute | solution.py:43
  545.5 88.9 %reduce-scatter.16.cloned.1.call-start = ((), (), s32[]{:S(2)}) async-start(), calls=%async_computation.13 | async-start | bytes 3145728 | tf_op jit(solution)/shard_map/reduce_scatter | solution.py:223
  548.4 142.5 %all-reduce.2.cloned.1.call-start = ((), (), s32[]{:S(2)}) async-start(), calls=%async_computation.16 | async-start | bytes 589824 | tf_op jit(solution)/shard_map/psum | solution.py:225
  548.4 65.3 %collective-permute-start.18 = (bf16[4,256,512]{2,1,0:T(8,128)(2,1)S(1)}, bf16[4,256,512]{2,1,0:T(8,128)(2,1)}, u32[]{:S(2)}, u32[]{:S(2)}) collective-permute-start(bf16[4,256,512]{2,1,0:T(8,128)(2,1)S(1)} %get-tuple-element.58), channel_id=1, source_target_pairs={{0,2},{1,3},{2,0},{3,1},{4,6},{5,7},{6,4},{7,5},{8,10},{9,11},{10,... | collective-permute-start | bytes 3145736 | tf_op jit(solution)/shard_map/ppermute | solution.py:43
  551.0 169.6 %reduce-scatter.20.cloned.1.call-start = ((), (), s32[]{:S(2)}) async-start(), calls=%async_computation.15 | async-start | bytes 1310720 | tf_op jit(solution)/shard_map/reduce_scatter | solution.py:227
  634.4 103.1 %all-gather.11.cloned.1.call-start = ((), (), s32[]{:S(2)}) async-start(), calls=%async_computation.18 | async-start | bytes 1310720 | tf_op jit(solution)/shard_map/all_gather | solution.py:228
  635.2 120.5 %all-gather.9.cloned.1.call-start = ((), (), s32[]{:S(2)}) async-start(), calls=%async_computation.17 | async-start | bytes 1310720 | tf_op jit(solution)/shard_map/all_gather | solution.py:230
  635.2 25.8 %collective-permute-start.19 = (bf16[4,256,512]{2,1,0:T(8,128)(2,1)S(1)}, bf16[4,256,512]{2,1,0:T(8,128)(2,1)S(1)}, u32[]{:S(2)}, u32[]{:S(2)}) collective-permute-start(bf16[4,256,512]{2,1,0:T(8,128)(2,1)S(1)} %get-tuple-element.57), channel_id=1, source_target_pairs={{0,3},{1,0},{2,1},{3,2},{4,7},{5,4},{6,5},{7,6},{8,11},{9,8},{10,9... | collective-permute-start | bytes 3145736 | tf_op jit(solution)/shard_map/ppermute | solution.py:43
  661.0 68.7 %copy-start.24 = (bf16[4,256,512]{2,1,0:T(8,128)(2,1)}, bf16[4,256,512]{2,1,0:T(8,128)(2,1)S(1)}, u32[]{:S(2)}) copy-start(bf16[4,256,512]{2,1,0:T(8,128)(2,1)S(1)} %collective-permute-done.19) | copy-start | bytes 3145732
  743.2 14.7 %copy-start.27 = (f32[512,512]{1,0:T(8,128)S(1)}, f32[512,512]{1,0:T(8,128)}, u32[]{:S(2)}) copy-start(f32[512,512]{1,0:T(8,128)} %all-gather.11.cloned.1.call-done) | copy-start | bytes 3145732
  743.2 15.7 %copy-start.1 = (bf16[1024,256]{1,0:T(8,128)(2,1)S(1)}, bf16[1024,256]{1,0:T(8,128)(2,1)}, u32[]{:S(2)}) copy-start(bf16[1024,256]{1,0:T(8,128)(2,1)} %param.6) | copy-start | bytes 1572868
  (15 other events, 42.6 us)
Sparse Core Ops, SparseCore 0:
  26.4 38.5 all-gather.4
  66.9 36.7 all-gather.6
  288.4 45.6 reduce-scatter.9
  404.3 50.7 reduce-scatter.13
  464.5 47.0 reduce-scatter.7
  513.6 31.8 reduce-scatter.11
  547.9 51.0 reduce-scatter.17
  601.9 32.5 reduce-scatter.15
  637.8 53.0 all-reduce.1
  693.2 27.3 reduce-scatter.19
  722.1 15.3 all-gather.10
  738.9 16.7 all-gather.8

commit v2 on v1

--- a/solution.py
+++ b/solution.py
@@ -14,17 +14,27 @@
     return logistic * (1.0 + values * (1.0 - logistic))
 
 
-def to_pixels(block):
+def sent_pixels(block):
     count = lax.axis_size("filt")
     me = lax.axis_index("filt")
     rows, cols, chans = block.shape
     share = cols // count
-    out = jnp.zeros((rows, share, chans * count), block.dtype)
+    pieces = []
     for step in range(count):
         target = lax.rem(me + step, count)
         piece = lax.dynamic_slice(block, (0, target * share, 0), (rows, share, chans))
         if step:
             piece = lax.ppermute(piece, "filt", [(i, (i + step) % count) for i in range(count)])
+        pieces.append(piece)
+    return pieces
+
+
+def all_channels(pieces):
+    count = lax.axis_size("filt")
+    me = lax.axis_index("filt")
+    rows, share, chans = pieces[0].shape
+    out = jnp.zeros((rows, share, chans * count), pieces[0].dtype)
+    for step, piece in enumerate(pieces):
         source = lax.rem(me + count - step, count)
         out = lax.dynamic_update_slice(out, piece, (0, 0, source * chans))
     return out
@@ -63,11 +73,19 @@
     return out
 
 
-def whole_weight(shard):
+def weight_part(shard):
     part = shard.shape[0] // lax.axis_size("rows")
     piece = lax.dynamic_slice_in_dim(shard, lax.axis_index("rows") * part, part, axis=0)
-    piece = lax.all_gather(piece, "filt", axis=1, tiled=True)
-    return lax.all_gather(piece, ("chan", "rows"), axis=0, tiled=True)
+    return lax.all_gather(piece, "filt", axis=1, tiled=True)
+
+
+def chan_sum(values):
+    if lax.axis_size("chan") != 2:
+        return lax.psum_scatter(values, "chan", scatter_dimension=0, tiled=True)
+    me, half = lax.axis_index("chan"), values.shape[0] // 2
+    other = lax.dynamic_slice_in_dim(values, (1 - me) * half, half, axis=0)
+    other = lax.ppermute(other, "chan", [(0, 1), (1, 0)])
+    return lax.dynamic_slice_in_dim(values, me * half, half, axis=0) + other
 
 
 def summed_rows(partial):
@@ -137,16 +155,20 @@
 
 def body(images, first_weight, group_weight, third_weight, out_grad):
     group_size = group_weight.shape[2]
-    first_panel = whole_weight(first_weight)
+    image_pieces = sent_pixels(images)
+    kernel = lax.all_gather(group_weight, "filt", axis=3, tiled=True)
+    kernel, first_part, third_part = hold(
+        image_pieces, 1, kernel, weight_part(first_weight), weight_part(third_weight)
+    )
+    first_panel = lax.all_gather(first_part, ("chan", "rows"), axis=0, tiled=True)
     mid = first_panel.shape[1]
     count = mid // BLOCK
-    image_pixels = to_pixels(images)
+    image_pixels = all_channels(image_pieces)
     rows, share, whole = image_pixels.shape
     pixels = rows * share
     out_grad_later, image_pixels = lax.optimization_barrier((out_grad, image_pixels))
-    grad_pixels = to_pixels(out_grad_later)
-    third_panel = whole_weight(third_weight)
-    kernel = lax.all_gather(group_weight, "filt", axis=3, tiled=True)
+    grad_pixels = all_channels(sent_pixels(out_grad_later))
+    third_panel = lax.all_gather(third_part, ("chan", "rows"), axis=0, tiled=True)
     panels, turned = block_kernels(kernel)
 
     flat_images = image_pixels.reshape(pixels, whole)
@@ -187,9 +209,8 @@
     third_part = lax.dot_general(
         act_group, flat_grad, (((0,), (0,)), ((), ())), preferred_element_type=jnp.float32
     )
-    third_sum = summed_rows(third_part).astype(jnp.float32)
-    third_sum = lax.psum_scatter(third_sum, "chan", scatter_dimension=0, tiled=True)
-    delta_windows = hold(block_pieces, 2, *delta_windows)
+    *delta_windows, third_sum = hold(block_pieces, 2, *delta_windows, summed_rows(third_part))
+    third_sum = chan_sum(third_sum.astype(jnp.float32))
 
     first_delta, kernel_part = pl.pallas_call(
         lambda *refs: backward_kernel(group_size, *refs),
@@ -206,7 +227,8 @@
         ),
     )(*windows, *delta_windows, turned, pre_first)
 
-    (first_delta,) = hold(block_pieces, 3, first_delta)
+    first_delta, third_sum = hold(block_pieces, 3, first_delta, third_sum)
+    third_sum = lax.psum_scatter(third_sum, "filt", scatter_dimension=1, tiled=True)
     block_out = placed(block_pieces)
     first_part = lax.dot_general(
         flat_images, first_delta, (((0,), (0,)), ((), ())), preferred_element_type=jnp.float32
@@ -216,17 +238,13 @@
     ).astype(jnp.bfloat16)
     back_pieces = sent_back(back_pixels.reshape(rows, share, whole))
     kernel_sum = lax.psum_scatter(kernel_part, "filt", scatter_dimension=2, tiled=True)
-    first_sum, third_sum, kernel_sum = hold(
-        back_pieces, 1, summed_rows(first_part), third_sum, kernel_sum
-    )
-    first_sum = first_sum.astype(jnp.float32)
-    first_sum = lax.psum_scatter(first_sum, "chan", scatter_dimension=0, tiled=True)
-    third_sum = lax.psum_scatter(third_sum, "filt", scatter_dimension=1, tiled=True)
+    first_sum, third_sum = hold(back_pieces, 1, summed_rows(first_part), third_sum)
+    first_sum = chan_sum(first_sum.astype(jnp.float32))
+    third_grad = lax.all_gather(third_sum, "rows", axis=0, tiled=True)
+    first_sum, kernel_sum = hold(back_pieces, 2, first_sum, kernel_sum)
+    first_sum = lax.psum_scatter(first_sum, "filt", scatter_dimension=1, tiled=True)
     kernel_sum = lax.psum(kernel_sum, ("rows", "chan"))
-    first_sum, third_sum = hold(back_pieces, 2, first_sum, third_sum)
-    first_sum = lax.psum_scatter(first_sum, "filt", scatter_dimension=1, tiled=True)
-    third_grad = lax.all_gather(third_sum, "rows", axis=0, tiled=True)
-    first_sum, kernel_sum = hold(back_pieces, 3, first_sum, kernel_sum)
+    (first_sum,) = hold(back_pieces, 3, first_sum)
     first_grad = lax.all_gather(first_sum, "rows", axis=0, tiled=True)
     back_images = placed(back_pieces)
     images_grad = out_grad.astype(jnp.float32) + back_images.astype(jnp.float32)

time: 775 us -> 727 us (0.938)
  blocking collectives: 122 us -> 69.3 us
  waiting for transfers between devices: 402 us -> 359 us
  starting transfers between devices: 58.3 us -> 92.5 us
  local copies, waits for them, and re-layouts: 71.5 us -> 80.5 us
    all_gather x1, blocking collectives: 86.9 us -> 17.2 us  [body(): kernel = lax.all_gather(group_weight, 'filt', axis=3, tiled=True)]
    reduce_scatter x2 -> x0, waiting for transfers between devices: 54.7 us -> none  [the longest x1 34 us: body(): lax.psum_scatter(third_sum, 'chan', scatter_dimension=0, tiled=True)]
    ppermute x6, waiting for transfers between devices: 195 us -> 151 us  [sent_back(): lax.ppermute(piece, 'filt', [(i, (i + step) % count) for i in range(count)])]
    ppermute x6 -> x8, waiting for transfers between devices: 59.8 us -> 98.3 us  [the longest x6 76.9 us: sent_pixels(): lax.ppermute(piece, 'filt', [(i, (i + step) % count) for i in range(count)])]
    reduce_scatter x1, waiting for transfers between devices: 29.6 us -> 0.01 us  [body(): lax.psum_scatter(first_sum, 'filt', scatter_dimension=1, tiled=True)]
    psum x1, waiting for transfers between devices: 29.9 us -> 56.6 us  [body(): kernel_sum = lax.psum(kernel_sum, ('rows', 'chan'))]
    ppermute x4, starting transfers between devices: 13.5 us -> 33 us  [edges(): lax.ppermute(last, axis, forward)]
    reduce_scatter x2, waiting for transfers between devices: 6.71 us -> 24.6 us  [summed_rows(): return lax.psum_scatter(split, 'rows', scatter_dimension=0, tiled=True)]
  transfers between devices with their start and end apart: 32 -> 32, of which waited for: 17 -> 17; matrix products, arithmetic and copies ran while one was open for 17% -> 18% of each run, Pallas kernels for 3% -> 3%
where the time goes in v2:
time: 727 us; the launch traced here: 718 us
  waiting for transfers between devices  359 us (49%)
  starting transfers between devices  92.5 us (13%)
  local copies, waits for them, and re-layouts  80.5 us (11%)
  blocking collectives  69.3 us (10%)
  matrix products  43.5 us (6%)
  other arithmetic  33.3 us (5%)
  Pallas kernels  25 us (3%)
  between operations  15.2 us (2%)
    ppermute x6, waiting for transfers between devices, sent_back(): lax.ppermute(piece, 'filt', [(i, (i + step) % count) for i in range(count)])  151 us
    ppermute x6, waiting for transfers between devices, sent_pixels(): lax.ppermute(piece, 'filt', [(i, (i + step) % count) for i in range(count)])  76.9 us
    psum x1, waiting for transfers between devices, body(): kernel_sum = lax.psum(kernel_sum, ('rows', 'chan'))  56.6 us
    all_gather x2, blocking collectives, weight_part(): return lax.all_gather(piece, 'filt', axis=1, tiled=True)  52.1 us
    ppermute x6, starting transfers between devices, sent_pixels(): lax.ppermute(piece, 'filt', [(i, (i + step) % count) for i in range(count)])  37.1 us
    ppermute x4, starting transfers between devices, edges(): lax.ppermute(last, axis, forward)  33 us
    reduce_scatter x2, waiting for transfers between devices, summed_rows(): return lax.psum_scatter(split, 'rows', scatter_dimension=0, tiled=True)  24.6 us
    unnamed x69, local copies, waits for them, and re-layouts  23.2 us
  transfers between devices with their start and end apart: 32, of which 17 were waited for; matrix products, arithmetic and copies ran while one was open for 18% of the time, Pallas kernels for 3%

profile of v2, /device:TPU:0, one launch (start us, length us, event | category | flops | bytes accessed | tf_op | source)
XLA Modules:
  0.0 718.0 jit_solution(1860677073017448969)
XLA Ops:
  13.3 3.0 collective-permute-start
  17.2 36.3 %all_gather.22 = bf16[256,1024]{1,0:T(8,128)(2,1)} all-gather(bf16[256,256]{1,0:T(8,128)(2,1)S(1)} %constant_dynamic-slice_fusion.13), channel_id=1, replica_groups=mesh['rows'=4,'chan'=2,'filt'=4] {'filt'}, dimensions={1}, use_global_device_ids=true | all-gather | bytes 655360 | tf_op jit(solution)/shard_map/all_gather | solution.py:79
  53.5 15.8 %all_gather.23 = bf16[128,2048]{1,0:T(8,128)(2,1)} all-gather(bf16[128,512]{1,0:T(8,128)(2,1)S(1)} %constant_dynamic-slice_fusion.12), channel_id=1, replica_groups=mesh['rows'=4,'chan'=2,'filt'=4] {'filt'}, dimensions={1}, use_global_device_ids=true | all-gather | bytes 655360 | tf_op jit(solution)/shard_map/all_gather | solution.py:79
  69.4 17.2 %all_gather.21 = bf16[3,3,32,1024]{3,2,1,0:T(8,128)(2,1)S(1)} all-gather(bf16[3,3,32,256]{3,2,1,0:T(8,128)(2,1)S(1)} %copy-done.30), channel_id=1, replica_groups=mesh['rows'=4,'chan'=2,'filt'=4] {'filt'}, dimensions={3}, use_global_device_ids=true | all-gather | bytes 737280 | tf_op jit(solution)/shard_map/all_gather | solution.py:159
  87.4 9.5 %collective-permute-start.1 = (bf16[4,256,512]{2,1,0:T(8,128)(2,1)}, bf16[4,256,512]{2,1,0:T(8,128)(2,1)}, u32[]{:S(2)}, u32[]{:S(2)}) collective-permute-start(bf16[4,256,512]{2,1,0:T(8,128)(2,1)} %get-tuple-element.80), channel_id=1, source_target_pairs={{0,2},{1,3},{2,0},{3,1},{4,6},{5,7},{6,4},{7,5},{8,10},{9,11},{10,... | collective-permute-start | bytes 3145736 | tf_op jit(solution)/shard_map/ppermute | solution.py:27
  96.9 3.5 collective-permute-start.2
  100.4 2.4 constant_dynamic-update-slice_fusion.11
  102.8 29.7 %collective-permute-done.1 = bf16[4,256,512]{2,1,0:T(8,128)(2,1)} collective-permute-done((bf16[4,256,512]{2,1,0:T(8,128)(2,1)}, bf16[4,256,512]{2,1,0:T(8,128)(2,1)}, u32[]{:S(2)}, u32[]{:S(2)}) %collective-permute-start.1) | collective-permute-done | bytes 1048608 | tf_op jit(solution)/shard_map/ppermute | solution.py:27
  141.5 17.6 %collective-permute-start.8 = (bf16[4,256,512]{2,1,0:T(8,128)(2,1)}, bf16[4,256,512]{2,1,0:T(8,128)(2,1)}, u32[]{:S(2)}, u32[]{:S(2)}) collective-permute-start(bf16[4,256,512]{2,1,0:T(8,128)(2,1)} %get-tuple-element.75), channel_id=1, source_target_pairs={{0,1},{1,2},{2,3},{3,0},{4,5},{5,6},{6,7},{7,4},{8,9},{9,10},{10,1... | collective-permute-start | bytes 3145736 | tf_op jit(solution)/shard_map/ppermute | solution.py:27
  159.1 3.4 collective-permute-start.9
  162.5 10.4 %multiply_convert_fusion.1 = (bf16[1024,1024]{1,0:T(8,128)(2,1)S(1)}, f32[1024,1024]{1,0:T(8,128)}) fusion(bf16[1024,2048]{1,0:T(8,128)(2,1)} %bitcast.62, bf16[2048,1024]{1,0:T(8,128)(2,1)} %all-gather.5.cloned.1.call-done), kind=kOutput, calls=%fused_computation.5 | convolution fusion | flops 4300210176 | bytes 14680064 | tf_op jit(solution)/shard_map/dot_general | solution.py:175
  178.3 2.9 bitcast_select_fusion.1.panel
  181.2 5.2 collective-permute-done.8
  188.0 42.0 %collective-permute-done.9 = bf16[4,256,512]{2,1,0:T(8,128)(2,1)} collective-permute-done((bf16[4,256,512]{2,1,0:T(8,128)(2,1)}, bf16[4,256,512]{2,1,0:T(8,128)(2,1)}, u32[]{:S(2)}, u32[]{:S(2)}) %collective-permute-start.9) | collective-permute-done | bytes 1048608 | tf_op jit(solution)/shard_map/ppermute | solution.py:27
  232.8 2.4 pad_maximum_fusion.s1.refs_1_
  238.1 24.2 %collective-permute-start.5 = (bf16[6,1,1024]{2,1,0:T(2,128)(2,1)S(1)}, bf16[6,1,1024]{2,1,0:T(2,128)(2,1)S(1)}, u32[]{:S(2)}, u32[]{:S(2)}) collective-permute-start(bf16[6,1,1024]{2,1,0:T(2,128)(2,1)S(1)} %get-tuple-element.88), channel_id=1, source_target_pairs={{0,1},{1,2},{2,3},{3,4},{4,5},{5,6},{6,7},{8,9},{9,10},{10,11},{11... | collective-permute-start | bytes 36872 | tf_op jit(solution)/shard_map/ppermute | solution.py:104
  264.7 9.9 %shard_map.92 = (f32[1024,1024]{1,0:T(8,128)}, bf16[1024,1024]{1,0:T(8,128)(2,1)S(1)}) custom-call(bf16[6,256,1024]{2,1,0:T(8,128)(2,1)S(1)} %pad_maximum_fusion.1.s0.refs_0_, bf16[6,256,1024]{2,1,0:T(8,128)(2,1)S(1)} %pad_maximum_fusion.s1.refs_1_, bf16[6,256,1024]{2,1,0:T(8,128)(2,1)S(1)} %pad_maximum_fusion.2.s2.refs_2_, ...), custom_call_target="tpu_custom_call" | custom-call | flops 4831838208 | bytes 41943040 | tf_op jit(solution)/shard_map/pallas_call | solution.py:183
  275.9 4.8 convolution_convert_fusion.2
  280.7 2.6 copy.17
  283.4 8.6 %add_convert_fusion = bf16[1024,2048]{1,0:T(8,128)(2,1)S(1)} fusion(bf16[1024,2048]{1,0:T(8,128)(2,1)} %bitcast.63, bf16[1024,1024]{1,0:T(8,128)(2,1)} %copy-done.6, bf16[1024,2048]{1,0:T(8,128)(2,1)} %all-gather.7.cloned.1.call-done), kind=kOutput, calls=%fused_computation.1 | convolution fusion | flops 4301258752 | bytes 14680064 | tf_op jit(solution)/shard_map/dot_general | solution.py:198
  294.2 2.4 copy-done.22
  299.9 5.7 multiply_convert_fusion
  305.6 17.2 %collective-permute-done.7 = bf16[4,256,512]{2,1,0:T(8,128)(2,1)S(1)} collective-permute-done((bf16[4,256,512]{2,1,0:T(8,128)(2,1)S(1)}, bf16[4,256,512]{2,1,0:T(8,128)(2,1)S(1)}, u32[]{:S(2)}, u32[]{:S(2)}) %collective-permute-start.7) | collective-permute-done | bytes 1048608 | tf_op jit(solution)/shard_map/ppermute | solution.py:53
  336.3 4.5 collective-permute-start.14
  342.9 9.2 %collective-permute-done.14 = bf16[6,1,1024]{2,1,0:T(2,128)(2,1)S(1)} collective-permute-done((bf16[6,1,1024]{2,1,0:T(2,128)(2,1)S(1)}, bf16[6,1,1024]{2,1,0:T(2,128)(2,1)S(1)}, u32[]{:S(2)}, u32[]{:S(2)}) %collective-permute-start.14) | collective-permute-done | bytes 12320 | tf_op jit(solution)/shard_map/ppermute | solution.py:104
  352.2 2.6 pad_maximum_fusion.4.refs_3_
  354.8 22.7 %collective-permute-done.11 = bf16[4,256,512]{2,1,0:T(8,128)(2,1)} collective-permute-done((bf16[4,256,512]{2,1,0:T(8,128)(2,1)}, bf16[4,256,512]{2,1,0:T(8,128)(2,1)}, u32[]{:S(2)}, u32[]{:S(2)}) %collective-permute-start.11) | collective-permute-done | bytes 1048608 | tf_op jit(solution)/shard_map/ppermute | solution.py:53
  381.3 2.8 collective-permute-start.17
  384.0 3.6 bitcast_select_fusion
  387.6 6.6 copy.18
  399.2 15.1 %shard_map.93 = (bf16[1024,1024]{1,0:T(8,128)(2,1)S(1)}, f32[9,32,1024]{2,1,0:T(8,128)}) custom-call(bf16[6,256,1024]{2,1,0:T(8,128)(2,1)S(1)} %copy-done.5, bf16[6,256,1024]{2,1,0:T(8,128)(2,1)S(1)} %pad_maximum_fusion.s1.refs_1_, bf16[6,256,1024]{2,1,0:T(8,128)(2,1)S(1)} %copy-done.3, bf16[6,256,1024]{2,1,0:T(8,128)(2,1)} %pad_maximum_fusion.4.refs_3_, ...), custom_call_target="tpu_custom_call" | custom-call | flops 9663676416 | bytes 62914560 | tf_op jit(solution)/shard_map/pallas_call | solution.py:215
  415.7 2.5 dynamic-slice_add_fusion.1
  418.1 5.2 collective-permute-done.16
  423.4 7.0 convolution_convert_fusion
  430.5 2.5 copy.19
  433.2 7.0 convolution_convert_fusion.1
  446.2 25.6 %collective-permute-done.18 = bf16[4,256,512]{2,1,0:T(8,128)(2,1)S(1)} collective-permute-done((bf16[4,256,512]{2,1,0:T(8,128)(2,1)S(1)}, bf16[4,256,512]{2,1,0:T(8,128)(2,1)S(1)}, u32[]{:S(2)}, u32[]{:S(2)}) %collective-permute-start.18) | collective-permute-done | bytes 1048608 | tf_op jit(solution)/shard_map/ppermute | solution.py:53
  472.8 24.6 %reduce-scatter.8.cloned.1.call-done = bf16[512,1024]{1,0:T(8,128)(2,1)} async-done(((bf16[2048,1024]{1,0:T(8,128)(2,1)}), bf16[512,1024]{1,0:T(8,128)(2,1)}) %reduce-scatter.8.cloned.1.call-update) | async-done | bytes 1048592 | tf_op jit(solution)/shard_map/reduce_scatter | solution.py:96
  501.4 2.4 collective-permute-start.19
  503.8 21.3 %collective-permute-done.20 = f32[256,1024]{1,0:T(8,128)} collective-permute-done((f32[256,1024]{1,0:T(8,128)}, f32[256,1024]{1,0:T(8,128)}, u32[]{:S(2)}, u32[]{:S(2)}) %collective-permute-start.20) | collective-permute-done | bytes 1048608 | tf_op jit(solution)/shard_map/ppermute | solution.py:87
  527.5 41.2 %collective-permute-done.19 = bf16[4,256,512]{2,1,0:T(8,128)(2,1)} collective-permute-done((bf16[4,256,512]{2,1,0:T(8,128)(2,1)}, bf16[4,256,512]{2,1,0:T(8,128)(2,1)}, u32[]{:S(2)}, u32[]{:S(2)}) %collective-permute-start.19) | collective-permute-done | bytes 1048608 | tf_op jit(solution)/shard_map/ppermute | solution.py:53
  569.5 3.4 collective-permute-start.21
  572.8 39.5 %collective-permute-done.21 = bf16[4,256,512]{2,1,0:T(8,128)(2,1)S(1)} collective-permute-done((bf16[4,256,512]{2,1,0:T(8,128)(2,1)S(1)}, bf16[4,256,512]{2,1,0:T(8,128)(2,1)S(1)}, u32[]{:S(2)}, u32[]{:S(2)}) %collective-permute-start.21) | collective-permute-done | bytes 1048608 | tf_op jit(solution)/shard_map/ppermute | solution.py:53
  612.4 2.6 constant_dynamic-update-slice_fusion.4
  625.8 5.0 all-gather.11.cloned.1.call-done
  631.9 8.3 %convert_add_fusion = f32[4,1024,512]{2,1,0:T(8,128)} fusion(bf16[4,1024,512]{2,1,0:T(8,128)(2,1)} %constant_dynamic-update-slice_fusion.1, bf16[4,1024,512]{2,1,0:T(8,128)(2,1)} %param.9), kind=kLoop, calls=%fused_computation | loop fusion | flops 6291456 | bytes 16777216 | tf_op jit(solution)/shard_map/add | solution.py:250
  640.1 9.0 %all-gather.9.cloned.1.call-done = f32[1024,256]{1,0:T(8,128)} async-done(((f32[256,256]{1,0:T(8,128)}), f32[1024,256]{1,0:T(8,128)}) %all-gather.9.cloned.1.call-update) | async-done | bytes 1048592 | tf_op jit(solution)/shard_map/all_gather | solution.py:248
  649.1 56.6 %all-reduce.2.cloned.1.call-done = f32[3,3,32,256]{3,2,1,0:T(8,128)} async-done(((f32[3,3,32,256]{3,2,1,0:T(8,128)}), f32[3,3,32,256]{3,2,1,0:T(8,128)}) %all-reduce.2.cloned.1.call-update) | async-done | bytes 294928 | tf_op jit(solution)/shard_map/psum | solution.py:246
  (160 shorter events, 95.3 us)
Async XLA Ops:
  7.2 9.1 %copy-start = (bf16[1024,256]{1,0:T(8,128)(2,1)S(1)}, bf16[1024,256]{1,0:T(8,128)(2,1)}, u32[]{:S(2)}) copy-start(bf16[1024,256]{1,0:T(8,128)(2,1)} %param.6) | copy-start | bytes 1572868
  7.2 155.3 %all-gather.5.cloned.1.call-start = ((), (), s32[]{:S(2)}) async-start(), calls=%async_computation.5 | async-start | bytes 4718592 | tf_op jit(solution)/shard_map/all_gather | solution.py:163
  9.5 59.9 %copy-start.30 = (bf16[3,3,32,256]{3,2,1,0:T(8,128)(2,1)S(1)}, bf16[3,3,32,256]{3,2,1,0:T(8,128)(2,1)}, u32[]{:S(2)}) copy-start(bf16[3,3,32,256]{3,2,1,0:T(8,128)(2,1)} %param.7) | copy-start | bytes 442372
  13.3 73.3 %collective-permute-start = (bf16[4,256,512]{2,1,0:T(8,128)(2,1)}, bf16[4,256,512]{2,1,0:T(8,128)(2,1)}, u32[]{:S(2)}, u32[]{:S(2)}) collective-permute-start(bf16[4,256,512]{2,1,0:T(8,128)(2,1)} %get-tuple-element.78), channel_id=1, source_target_pairs={{0,1},{1,2},{2,3},{3,0},{4,5},{5,6},{6,7},{7,4},{8,9},{9,10},{10,1... | collective-permute-start | bytes 3145736 | tf_op jit(solution)/shard_map/ppermute | solution.py:27
  86.6 196.9 %all-gather.7.cloned.1.call-start = ((), (), s32[]{:S(2)}) async-start(), calls=%async_computation.6 | async-start | bytes 4718592 | tf_op jit(solution)/shard_map/all_gather | solution.py:171
  87.3 290.1 %reduce-scatter.6.cloned.1.call-start = ((), (), s32[]{:S(2)}) async-start(), calls=%async_computation.7 | async-start | bytes 5242880 | tf_op jit(solution)/shard_map/reduce_scatter | solution.py:96
  87.4 45.2 %collective-permute-start.1 = (bf16[4,256,512]{2,1,0:T(8,128)(2,1)}, bf16[4,256,512]{2,1,0:T(8,128)(2,1)}, u32[]{:S(2)}, u32[]{:S(2)}) collective-permute-start(bf16[4,256,512]{2,1,0:T(8,128)(2,1)} %get-tuple-element.80), channel_id=1, source_target_pairs={{0,2},{1,3},{2,0},{3,1},{4,6},{5,7},{6,4},{7,5},{8,10},{9,11},{10,... | collective-permute-start | bytes 3145736 | tf_op jit(solution)/shard_map/ppermute | solution.py:27
  96.9 38.0 %collective-permute-start.2 = (bf16[4,256,512]{2,1,0:T(8,128)(2,1)S(1)}, bf16[4,256,512]{2,1,0:T(8,128)(2,1)}, u32[]{:S(2)}, u32[]{:S(2)}) collective-permute-start(bf16[4,256,512]{2,1,0:T(8,128)(2,1)S(1)} %get-tuple-element.77), channel_id=1, source_target_pairs={{0,3},{1,0},{2,1},{3,2},{4,7},{5,4},{6,5},{7,6},{8,11},{9,8},{10,9... | collective-permute-start | bytes 3145736 | tf_op jit(solution)/shard_map/ppermute | solution.py:27
  102.8 34.9 %copy-start.10 = (bf16[4,1024,512]{2,1,0:T(8,128)(2,1)S(1)}, bf16[4,1024,512]{2,1,0:T(8,128)(2,1)}, u32[]{:S(2)}) copy-start(bf16[4,1024,512]{2,1,0:T(8,128)(2,1)} %param.9) | copy-start | bytes 12582916
  141.5 45.0 %collective-permute-start.8 = (bf16[4,256,512]{2,1,0:T(8,128)(2,1)}, bf16[4,256,512]{2,1,0:T(8,128)(2,1)}, u32[]{:S(2)}, u32[]{:S(2)}) collective-permute-start(bf16[4,256,512]{2,1,0:T(8,128)(2,1)} %get-tuple-element.75), channel_id=1, source_target_pairs={{0,1},{1,2},{2,3},{3,0},{4,5},{5,6},{6,7},{7,4},{8,9},{9,10},{10,1... | collective-permute-start | bytes 3145736 | tf_op jit(solution)/shard_map/ppermute | solution.py:27
  159.1 70.9 %collective-permute-start.9 = (bf16[4,256,512]{2,1,0:T(8,128)(2,1)}, bf16[4,256,512]{2,1,0:T(8,128)(2,1)}, u32[]{:S(2)}, u32[]{:S(2)}) collective-permute-start(bf16[4,256,512]{2,1,0:T(8,128)(2,1)} %get-tuple-element.74), channel_id=1, source_target_pairs={{0,2},{1,3},{2,0},{3,1},{4,6},{5,7},{6,4},{7,5},{8,10},{9,11},{10,... | collective-permute-start | bytes 3145736 | tf_op jit(solution)/shard_map/ppermute | solution.py:27
  162.5 68.9 %collective-permute-start.10 = (bf16[4,256,512]{2,1,0:T(8,128)(2,1)}, bf16[4,256,512]{2,1,0:T(8,128)(2,1)}, u32[]{:S(2)}, u32[]{:S(2)}) collective-permute-start(bf16[4,256,512]{2,1,0:T(8,128)(2,1)} %get-tuple-element.73), channel_id=1, source_target_pairs={{0,3},{1,0},{2,1},{3,2},{4,7},{5,4},{6,5},{7,6},{8,11},{9,8},{10,9... | collective-permute-start | bytes 3145736 | tf_op jit(solution)/shard_map/ppermute | solution.py:27
  172.9 8.3 %copy-start.14 = (bf16[1024,1024]{1,0:T(8,128)(2,1)}, bf16[1024,1024]{1,0:T(8,128)(2,1)S(1)}, u32[]{:S(2)}) copy-start(bf16[1024,1024]{1,0:T(8,128)(2,1)S(1)} %get-tuple-element.93) | copy-start | bytes 6291460
  174.1 58.7 %collective-permute-start.3 = (bf16[1,256,1024]{2,1,0:T(8,128)(2,1)}, bf16[1,256,1024]{2,1,0:T(8,128)(2,1)}, u32[]{:S(2)}, u32[]{:S(2)}) collective-permute-start(bf16[1,256,1024]{2,1,0:T(8,128)(2,1)} %get-tuple-element.91), channel_id=1, source_target_pairs={{0,8},{8,16},{16,24},{1,9},{9,17},{17,25},{2,10},{10,18},{18,26},{... | collective-permute-start | bytes 1572872 | tf_op jit(solution)/shard_map/ppermute | solution.py:104
  176.2 56.6 %collective-permute-start.4 = (bf16[1,256,1024]{2,1,0:T(8,128)(2,1)}, bf16[1,256,1024]{2,1,0:T(8,128)(2,1)}, u32[]{:S(2)}, u32[]{:S(2)}) collective-permute-start(bf16[1,256,1024]{2,1,0:T(8,128)(2,1)} %get-tuple-element.92), channel_id=1, source_target_pairs={{8,0},{16,8},{24,16},{9,1},{17,9},{25,17},{10,2},{18,10},{26,18},{... | collective-permute-start | bytes 1572872 | tf_op jit(solution)/shard_map/ppermute | solution.py:104
  178.0 8.5 %copy-start.19 = (bf16[4,256,2048]{2,1,0:T(8,128)(2,1)S(1)}, bf16[4,256,2048]{2,1,0:T(8,128)(2,1)}, u32[]{:S(2)}) copy-start(bf16[4,256,2048]{2,1,0:T(8,128)(2,1)} %copy-done.18) | copy-start | bytes 12582916
  178.1 57.1 %copy-start.13 = (bf16[9,32,4,256]{3,1,0,2:T(8,128)(2,1)}, bf16[9,32,4,256]{3,1,0,2:T(8,128)(2,1)S(1)}, u32[]{:S(2)}) copy-start(bf16[9,32,4,256]{3,1,0,2:T(8,128)(2,1)S(1)} %copy.22) | copy-start | bytes 1769476
  186.5 46.4 %copy-start.15 = (bf16[1024,1024]{1,0:T(8,128)(2,1)S(1)}, bf16[1024,1024]{1,0:T(8,128)(2,1)}, u32[]{:S(2)}) copy-start(bf16[1024,1024]{1,0:T(8,128)(2,1)} %copy-done.14) | copy-start | bytes 6291460
  232.8 41.8 %copy-start.20 = (bf16[4,256,2048]{2,1,0:T(8,128)(2,1)}, bf16[4,256,2048]{2,1,0:T(8,128)(2,1)S(1)}, u32[]{:S(2)}) copy-start(bf16[4,256,2048]{2,1,0:T(8,128)(2,1)S(1)} %constant_dynamic-update-slice_fusion.5) | copy-start | bytes 12582916
  235.3 27.1 %collective-permute-start.6 = (bf16[6,1,1024]{2,1,0:T(2,128)(2,1)S(1)}, bf16[6,1,1024]{2,1,0:T(2,128)(2,1)S(1)}, u32[]{:S(2)}, u32[]{:S(2)}) collective-permute-start(bf16[6,1,1024]{2,1,0:T(2,128)(2,1)S(1)} %get-tuple-element.87), channel_id=1, source_target_pairs={{1,0},{2,1},{3,2},{4,3},{5,4},{6,5},{7,6},{9,8},{10,9},{11,10},{12... | collective-permute-start | bytes 36872 | tf_op jit(solution)/shard_map/ppermute | solution.py:104
  238.1 25.6 %collective-permute-start.5 = (bf16[6,1,1024]{2,1,0:T(2,128)(2,1)S(1)}, bf16[6,1,1024]{2,1,0:T(2,128)(2,1)S(1)}, u32[]{:S(2)}, u32[]{:S(2)}) collective-permute-start(bf16[6,1,1024]{2,1,0:T(2,128)(2,1)S(1)} %get-tuple-element.88), channel_id=1, source_target_pairs={{0,1},{1,2},{2,3},{3,4},{4,5},{5,6},{6,7},{8,9},{9,10},{10,11},{11... | collective-permute-start | bytes 36872 | tf_op jit(solution)/shard_map/ppermute | solution.py:104
  262.8 11.8 %copy-start.2 = (bf16[6,256,1024]{2,1,0:T(8,128)(2,1)}, bf16[6,256,1024]{2,1,0:T(8,128)(2,1)S(1)}, u32[]{:S(2)}) copy-start(bf16[6,256,1024]{2,1,0:T(8,128)(2,1)S(1)} %pad_maximum_fusion.2.s2.refs_2_) | copy-start | bytes 9437188
  264.7 9.9 %copy-start.4 = (bf16[6,256,1024]{2,1,0:T(8,128)(2,1)}, bf16[6,256,1024]{2,1,0:T(8,128)(2,1)S(1)}, u32[]{:S(2)}) copy-start(bf16[6,256,1024]{2,1,0:T(8,128)(2,1)S(1)} %pad_maximum_fusion.1.s0.refs_0_) | copy-start | bytes 9437188
  283.4 188.5 %reduce-scatter.10.cloned.1.call-start = ((), (), s32[]{:S(2)}) async-start(), calls=%async_computation.9 | async-start | bytes 1310720 | tf_op jit(solution)/shard_map/reduce_scatter | solution.py:231
  296.6 26.2 %collective-permute-start.7 = (bf16[4,256,512]{2,1,0:T(8,128)(2,1)S(1)}, bf16[4,256,512]{2,1,0:T(8,128)(2,1)S(1)}, u32[]{:S(2)}, u32[]{:S(2)}) collective-permute-start(bf16[4,256,512]{2,1,0:T(8,128)(2,1)S(1)} %get-tuple-element.71), channel_id=1, source_target_pairs={{0,1},{1,2},{2,3},{3,0},{4,5},{5,6},{6,7},{7,4},{8,9},{9,10},{10,1... | collective-permute-start | bytes 3145736 | tf_op jit(solution)/shard_map/ppermute | solution.py:53
  305.6 17.2 %copy-start.16 = (bf16[1024,1024]{1,0:T(8,128)(2,1)}, bf16[1024,1024]{1,0:T(8,128)(2,1)S(1)}, u32[]{:S(2)}) copy-start(bf16[1024,1024]{1,0:T(8,128)(2,1)S(1)} %multiply_convert_fusion) | copy-start | bytes 6291460
  324.2 4.8 collective-permute-start.12
  326.3 5.0 collective-permute-start.13
  327.8 49.6 %collective-permute-start.11 = (bf16[4,256,512]{2,1,0:T(8,128)(2,1)}, bf16[4,256,512]{2,1,0:T(8,128)(2,1)}, u32[]{:S(2)}, u32[]{:S(2)}) collective-permute-start(bf16[4,256,512]{2,1,0:T(8,128)(2,1)} %get-tuple-element.70), channel_id=1, source_target_pairs={{0,2},{1,3},{2,0},{3,1},{4,6},{5,7},{6,4},{7,5},{8,10},{9,11},{10,... | collective-permute-start | bytes 3145736 | tf_op jit(solution)/shard_map/ppermute | solution.py:53
  333.5 7.3 %collective-permute-start.15 = (bf16[6,1,1024]{2,1,0:T(2,128)(2,1)S(1)}, bf16[6,1,1024]{2,1,0:T(2,128)(2,1)S(1)}, u32[]{:S(2)}, u32[]{:S(2)}) collective-permute-start(bf16[6,1,1024]{2,1,0:T(2,128)(2,1)S(1)} %get-tuple-element.83), channel_id=1, source_target_pairs={{1,0},{2,1},{3,2},{4,3},{5,4},{6,5},{7,6},{9,8},{10,9},{11,10},{12... | collective-permute-start | bytes 36872 | tf_op jit(solution)/shard_map/ppermute | solution.py:104
  336.3 15.9 %collective-permute-start.14 = (bf16[6,1,1024]{2,1,0:T(2,128)(2,1)S(1)}, bf16[6,1,1024]{2,1,0:T(2,128)(2,1)S(1)}, u32[]{:S(2)}, u32[]{:S(2)}) collective-permute-start(bf16[6,1,1024]{2,1,0:T(2,128)(2,1)S(1)} %get-tuple-element.84), channel_id=1, source_target_pairs={{0,1},{1,2},{2,3},{3,4},{4,5},{5,6},{6,7},{8,9},{9,10},{10,11},{11... | collective-permute-start | bytes 36872 | tf_op jit(solution)/shard_map/ppermute | solution.py:104
  381.3 34.4 %collective-permute-start.17 = (f32[128,2048]{1,0:T(8,128)}, f32[128,2048]{1,0:T(8,128)}, u32[]{:S(2)}, u32[]{:S(2)}) collective-permute-start(f32[128,2048]{1,0:T(8,128)} %constant_dynamic-slice_fusion.2), channel_id=1, source_target_pairs={{0,4},{4,0},{1,5},{5,1},{2,6},{6,2},{3,7},{7,3},{8,12},{12,8},{9,1... | collective-permute-start | bytes 3145736 | tf_op jit(solution)/shard_map/ppermute | solution.py:87
  394.2 29.1 %collective-permute-start.16 = (bf16[4,256,512]{2,1,0:T(8,128)(2,1)}, bf16[4,256,512]{2,1,0:T(8,128)(2,1)}, u32[]{:S(2)}, u32[]{:S(2)}) collective-permute-start(bf16[4,256,512]{2,1,0:T(8,128)(2,1)} %get-tuple-element.69), channel_id=1, source_target_pairs={{0,3},{1,0},{2,1},{3,2},{4,7},{5,4},{6,5},{7,6},{8,11},{9,8},{10,9... | collective-permute-start | bytes 3145736 | tf_op jit(solution)/shard_map/ppermute | solution.py:53
  399.2 16.4 %copy-start.12 = (f32[256,2048]{1,0:T(8,128)S(1)}, f32[256,2048]{1,0:T(8,128)}, u32[]{:S(2)}) copy-start(f32[256,2048]{1,0:T(8,128)} %copy-done.11) | copy-start | bytes 6291460
  423.4 74.0 %reduce-scatter.8.cloned.1.call-start = ((), (), s32[]{:S(2)}) async-start(), calls=%async_computation.8 | async-start | bytes 5242880 | tf_op jit(solution)/shard_map/reduce_scatter | solution.py:96
  432.9 135.7 %reduce-scatter.12.cloned.1.call-start = ((), (), s32[]{:S(2)}) async-start(), calls=%async_computation.10 | async-start | bytes 1474560 | tf_op jit(solution)/shard_map/reduce_scatter | solution.py:240
  444.4 27.4 %collective-permute-start.18 = (bf16[4,256,512]{2,1,0:T(8,128)(2,1)S(1)}, bf16[4,256,512]{2,1,0:T(8,128)(2,1)S(1)}, u32[]{:S(2)}, u32[]{:S(2)}) collective-permute-start(bf16[4,256,512]{2,1,0:T(8,128)(2,1)S(1)} %get-tuple-element.67), channel_id=1, source_target_pairs={{0,1},{1,2},{2,3},{3,0},{4,5},{5,6},{6,7},{7,4},{8,9},{9,10},{10,1... | collective-permute-start | bytes 3145736 | tf_op jit(solution)/shard_map/ppermute | solution.py:53
  446.1 166.2 %reduce-scatter.14.cloned.1.call-start = ((), (), s32[]{:S(2)}) async-start(), calls=%async_computation.11 | async-start | bytes 1310720 | tf_op jit(solution)/shard_map/reduce_scatter | solution.py:245
  499.9 25.2 %collective-permute-start.20 = (f32[256,1024]{1,0:T(8,128)}, f32[256,1024]{1,0:T(8,128)}, u32[]{:S(2)}, u32[]{:S(2)}) collective-permute-start(f32[256,1024]{1,0:T(8,128)} %constant_dynamic-slice_fusion.15), channel_id=1, source_target_pairs={{0,4},{4,0},{1,5},{5,1},{2,6},{6,2},{3,7},{7,3},{8,12},{12,8},{9,1... | collective-permute-start | bytes 3145736 | tf_op jit(solution)/shard_map/ppermute | solution.py:87
  501.4 67.3 %collective-permute-start.19 = (bf16[4,256,512]{2,1,0:T(8,128)(2,1)}, bf16[4,256,512]{2,1,0:T(8,128)(2,1)}, u32[]{:S(2)}, u32[]{:S(2)}) collective-permute-start(bf16[4,256,512]{2,1,0:T(8,128)(2,1)} %get-tuple-element.66), channel_id=1, source_target_pairs={{0,2},{1,3},{2,0},{3,1},{4,6},{5,7},{6,4},{7,5},{8,10},{9,11},{10,... | collective-permute-start | bytes 3145736 | tf_op jit(solution)/shard_map/ppermute | solution.py:53
  527.5 92.1 %copy-start.26 = (bf16[4,256,512]{2,1,0:T(8,128)(2,1)S(1)}, bf16[4,256,512]{2,1,0:T(8,128)(2,1)}, u32[]{:S(2)}) copy-start(bf16[4,256,512]{2,1,0:T(8,128)(2,1)} %copy-done.25) | copy-start | bytes 3145732
  568.7 62.1 %all-gather.11.cloned.1.call-start = ((), (), s32[]{:S(2)}) async-start(), calls=%async_computation.14 | async-start | bytes 1310720 | tf_op jit(solution)/shard_map/all_gather | solution.py:243
  569.4 79.7 %all-gather.9.cloned.1.call-start = ((), (), s32[]{:S(2)}) async-start(), calls=%async_computation.12 | async-start | bytes 1310720 | tf_op jit(solution)/shard_map/all_gather | solution.py:248
  569.5 42.9 %collective-permute-start.21 = (bf16[4,256,512]{2,1,0:T(8,128)(2,1)S(1)}, bf16[4,256,512]{2,1,0:T(8,128)(2,1)S(1)}, u32[]{:S(2)}, u32[]{:S(2)}) collective-permute-start(bf16[4,256,512]{2,1,0:T(8,128)(2,1)S(1)} %get-tuple-element.65), channel_id=1, source_target_pairs={{0,3},{1,0},{2,1},{3,2},{4,7},{5,4},{6,5},{7,6},{8,11},{9,8},{10,9... | collective-permute-start | bytes 3145736 | tf_op jit(solution)/shard_map/ppermute | solution.py:53
  612.4 93.4 %all-reduce.2.cloned.1.call-start = ((), (), s32[]{:S(2)}) async-start(), calls=%async_computation.13 | async-start | bytes 589824 | tf_op jit(solution)/shard_map/psum | solution.py:246
  620.6 10.2 %copy-start.28 = (bf16[4,256,512]{2,1,0:T(8,128)(2,1)S(1)}, bf16[4,256,512]{2,1,0:T(8,128)(2,1)}, u32[]{:S(2)}) copy-start(bf16[4,256,512]{2,1,0:T(8,128)(2,1)} %copy-done.27) | copy-start | bytes 3145732
  631.9 77.9 %copy-start.29 = (f32[512,512]{1,0:T(8,128)S(1)}, f32[512,512]{1,0:T(8,128)}, u32[]{:S(2)}) copy-start(f32[512,512]{1,0:T(8,128)} %all-gather.11.cloned.1.call-done) | copy-start | bytes 3145732
  631.9 78.8 %copy-start.1 = (bf16[1024,256]{1,0:T(8,128)(2,1)S(1)}, bf16[1024,256]{1,0:T(8,128)(2,1)}, u32[]{:S(2)}) copy-start(bf16[1024,256]{1,0:T(8,128)(2,1)} %param.6) | copy-start | bytes 1572868
  (17 other events, 57.3 us)
Sparse Core Ops, SparseCore 0:
  86.7 44.9 all-gather.4
  133.6 36.7 all-gather.6
  283.5 48.1 reduce-scatter.5
  423.5 26.5 reduce-scatter.9
  453.1 44.2 reduce-scatter.7
  499.7 54.8 reduce-scatter.11
  568.8 42.2 reduce-scatter.13
  612.7 18.0 all-gather.10
  632.4 16.7 all-gather.8
  652.7 53.0 all-reduce.1
